TPU v7x, 32 devices: a whole 2x2x4 slice. The times are simulated.
32 devices in a mesh: dp: 8 (over z, core), tensor: 4 (over y, x).
Axes of the slice: x: 2, y: 2, z: 4, core: 2. Of those that a mesh axis runs over, the one named last changes fastest.
Arguments:
- tokens: bfloat16 [2048, 1536], P(('dp', 'tensor')), may hold values from -6 to 6
- cotangent: bfloat16 [2048, 1536], P(('dp', 'tensor')), may hold values from -6 to 6
- norm_gains: bfloat16 [4, 1536], replicated, may hold values from 0.5 to 1.5
- mix_in: bfloat16 [1536, 2, 3072], P(None, None, 'tensor'), may hold values from -0.15625 to 0.15625
- conv_weight: float32 [4, 3072], P(None, 'tensor'), may hold values from -3 to 3
- x_proj: bfloat16 [3072, 128], P('tensor'), may hold values from -0.109375 to 0.109375
- dt_proj: bfloat16 [96, 3072], P(None, 'tensor'), may hold values from -0.625 to 0.625
- dt_bias: float32 [3072], P('tensor'), may hold values from -4.5 to -1.5
- a_log: float32 [3072, 16], P('tensor'), may hold values from 0 to 2.77
- skip_gain: float32 [3072], P('tensor'), may hold values from 0.5 to 1.5
- mix_out: bfloat16 [3072, 1536], P('tensor'), may hold values from -0.109375 to 0.109375
- ffn_in: bfloat16 [1536, 2, 4096], P(None, None, 'tensor'), may hold values from -0.15625 to 0.15625
- ffn_out: bfloat16 [4096, 1536], P('tensor'), may hold values from -0.09375 to 0.09375
- attn_query: bfloat16 [1536, 1536], P(None, 'tensor'), may hold values from -0.15625 to 0.15625
- attn_keyval: bfloat16 [1536, 2, 512], P(None, None, 'tensor'), may hold values from -0.15625 to 0.15625
- attn_out: bfloat16 [1536, 1536], P('tensor'), may hold values from -1.25 to 1.25
- router: bfloat16 [1536, 16], replicated, may hold values from -0.15625 to 0.15625
- expert_in: bfloat16 [16, 1536, 2, 1024], P(None, None, None, 'tensor'), may hold values from -0.15625 to 0.15625
- expert_out: bfloat16 [16, 1024, 1536], P(None, 'tensor'), may hold values from -0.1875 to 0.1875
- routes: int32 [2048, 2], P('dp'), may hold values from 0 to 15, all different within a row; in each aligned block of 256 rows (0 to 255, 256 to 511, ...) at most 48 rows name the same one
Outputs:
- block_out: bfloat16 [2048, 1536], P(('dp', 'tensor'))
- tokens_grad: float32 [2048, 1536], P(('dp', 'tensor'))
- norm_gains_grad: float32 [4, 1536], P(None, 'dp')
- mix_in_grad: float32 [1536, 2, 3072], P('dp', None, 'tensor')
- conv_weight_grad: float32 [4, 3072], P(None, ('tensor', 'dp'))
- x_proj_grad: float32 [3072, 128], P('tensor', 'dp')
- dt_proj_grad: float32 [96, 3072], P('dp', 'tensor')
- dt_bias_grad: float32 [3072], P(('tensor', 'dp'))
- a_log_grad: float32 [3072, 16], P(('tensor', 'dp'))
- skip_gain_grad: float32 [3072], P(('tensor', 'dp'))
- mix_out_grad: float32 [3072, 1536], P('tensor', 'dp')
- ffn_in_grad: float32 [1536, 2, 4096], P('dp', None, 'tensor')
- ffn_out_grad: float32 [4096, 1536], P('tensor', 'dp')
- attn_query_grad: float32 [1536, 1536], P('dp', 'tensor')
- attn_keyval_grad: float32 [1536, 2, 512], P('dp', None, 'tensor')
- attn_out_grad: float32 [1536, 1536], P('tensor', 'dp')
- router_grad: float32 [1536, 16], P('dp')
- expert_in_grad: float32 [16, 1536, 2, 1024], P(None, 'dp', None, 'tensor')
- expert_out_grad: float32 [16, 1024, 1536], P(None, 'tensor', 'dp')
Inputs may be any that keep to these rules, and one draw needn't show every extreme that they name: `routes`: each row names two different experts; in each sequence's 256 rows no expert is named by more than 48 rows, a bound that some block reaches.
All inputs are finite; a program needn't handle non-finite values.
Results may differ from a plain program's by a relative error of at most 0.04.
Values may be sent and summed in bfloat16 or wider, within the bound.
No kernel may reach another device: no remote copies, remote signals or barrier semaphores. Data moves between devices by JAX's collectives and lax.ppermute only.
A program may use at most 448 MiB of HBM per device.

v0:
```python
import functools
import math

import jax
import jax.numpy as jnp
from jax import lax
from jax.experimental import pallas as pl
from jax.experimental.pallas import tpu as pltpu
from jax.sharding import PartitionSpec as P

D = 1536
STATE = 16
CONV = 4
DT_RANK = 96
HEADS = 24
KV_HEADS = 8
HEAD_DIM = 64
EXPERTS = 16
LEN = 256
CAP = 48

epsilon = 1e-06
floor_square = 0.1
masked_score = -1e30
LOG2E = 1.4426950408889634
PAD = 8
CHUNK = 16
GROUP = 8
VMEM_LIMIT = 56 * 1024 * 1024

f32 = jnp.float32
bf16 = jnp.bfloat16


def matmul(left, right):
    return jnp.dot(left, right, preferred_element_type=f32)


def times_transposed(left, right):
    return lax.dot_general(left, right, (((1,), (1,)), ((), ())), preferred_element_type=f32)


def transposed_times(left, right):
    return lax.dot_general(left, right, (((0,), (0,)), ((), ())), preferred_element_type=f32)


def sigmoid(v):
    return 1.0 / (1.0 + jnp.exp(-v))


def dot_exact(left, right):
    return jnp.dot(left, right, precision=lax.Precision.HIGHEST, preferred_element_type=f32)


def column_norm_parts(projected):
    lane = lax.broadcasted_iota(jnp.int32, projected.shape, 1)
    square = projected * projected
    in_step = lane < DT_RANK
    in_b = jnp.logical_and(lane >= DT_RANK, lane < DT_RANK + STATE)
    in_c = lane >= DT_RANK + STATE
    mean_step = jnp.sum(jnp.where(in_step, square, 0.0), axis=1, keepdims=True) / DT_RANK
    mean_b = jnp.sum(jnp.where(in_b, square, 0.0), axis=1, keepdims=True) / STATE
    mean_c = jnp.sum(jnp.where(in_c, square, 0.0), axis=1, keepdims=True) / STATE
    r_step = lax.rsqrt(mean_step + epsilon)
    r_b = lax.rsqrt(jnp.maximum(mean_b, floor_square))
    r_c = lax.rsqrt(jnp.maximum(mean_c, floor_square))
    scale = jnp.where(in_step, r_step, jnp.where(in_b, r_b, r_c))
    return scale, in_step, in_b, in_c, mean_b, mean_c


def row_spread(cols_ref, first, out_ref):
    pick = (
        lax.broadcasted_iota(jnp.int32, (128, CHUNK * STATE), 0) - first
        == lax.broadcasted_iota(jnp.int32, (128, CHUNK * STATE), 1) % STATE
    ).astype(f32)
    out_ref[...] = (dot_exact(cols_ref[...], pick) * chunk_mask(LEN)).astype(bf16)


def chunk_mask(rows):
    return (
        lax.broadcasted_iota(jnp.int32, (rows, CHUNK * STATE), 0) % CHUNK
        == lax.broadcasted_iota(jnp.int32, (rows, CHUNK * STATE), 1) // STATE
    ).astype(f32)


def conv_total(pad_ref, weight_ref, length):
    total = weight_ref[0:1, :] * pad_ref[pl.ds(PAD - CONV + 1, length), :]
    for tap in range(1, CONV):
        total = total + weight_ref[tap : tap + 1, :] * pad_ref[pl.ds(PAD - CONV + 1 + tap, length), :]
    return total


def conv_forward_kernel(blocks, me_ref, xz_ref, weight_ref, xproj_ref, u_ref, proj_ref, pad_ref):
    me = me_ref[0]
    size = LEN // blocks
    pad_ref[0:PAD, :] = jnp.zeros((PAD, pad_ref.shape[1]), f32)
    for m in range(blocks):
        at = pl.multiple_of(jnp.bitwise_xor(me, m) * size, size)
        pad_ref[PAD + m * size : PAD + (m + 1) * size, :] = xz_ref[0, pl.ds(at, size), :]
    total = conv_total(pad_ref, weight_ref, LEN)
    u = total * sigmoid(total)
    for m in range(blocks):
        at = pl.multiple_of(jnp.bitwise_xor(me, m) * size, size)
        u_ref[pl.ds(at, size), :] = u[m * size : (m + 1) * size, :]
    proj_ref[...] = matmul(u_ref[...].astype(bf16), xproj_ref[...])


def scan_setup(proj_ref, cols_ref, b_ref, c_ref):
    projected = proj_ref[...]
    scale = column_norm_parts(projected)[0]
    cols_ref[...] = projected * scale
    row_spread(cols_ref, DT_RANK, b_ref)
    row_spread(cols_ref, DT_RANK + STATE, c_ref)


def step_sizes(cols_ref, dt_proj_ref, bias_ref):
    low = cols_ref[:, :DT_RANK].astype(bf16)
    pre = matmul(low, dt_proj_ref[...]) + bias_ref[...]
    return low, pre, jnp.maximum(pre, 0.0) + jnp.log1p(jnp.exp(-jnp.abs(pre)))


def chunk_place(index, me, size):
    block = index // (size // CHUNK)
    inner = index % (size // CHUNK)
    return pl.multiple_of(jnp.bitwise_xor(block, me) * size + inner * CHUNK, CHUNK)


def chunk_group(index):
    out = []
    for q in range(GROUP):
        base = (index * GROUP + q) * CHUNK
        out.append(
            (
                pl.ds(pl.multiple_of(base, CHUNK), CHUNK),
                pl.ds(pl.multiple_of(base * STATE, CHUNK * STATE), CHUNK * STATE),
            )
        )
    return out


def push_chunks(left_ref, right_ref, out_ref):
    def body(index, carry):
        for rows, many in chunk_group(index):
            out_ref[many, :] = transposed_times(left_ref[rows, :], right_ref[rows, :])
        return carry

    lax.fori_loop(0, LEN // CHUNK // GROUP, body, 0)


def scan_forward_kernel(
    blocks,
    me_ref,
    proj_ref,
    dt_proj_ref,
    bias_ref,
    alog_ref,
    skip_ref,
    u_ref,
    xz_ref,
    out_w_ref,
    gated_ref,
    ys_ref,
    states_ref,
    *rest,
):
    out_refs = rest[:blocks]
    cols_ref, b_ref, c_ref, delta_ref, drive_ref, push_ref, total_ref = rest[blocks:]
    me = me_ref[0]
    size = LEN // blocks
    lanes = u_ref.shape[1]
    step = pl.program_id(0)

    @pl.when(step == 0)
    def _():
        scan_setup(proj_ref, cols_ref, b_ref, c_ref)

    _, _, delta = step_sizes(cols_ref, dt_proj_ref, bias_ref)
    delta_ref[...] = delta
    drive_ref[...] = (delta * u_ref[...]).astype(bf16)
    rate = -jnp.exp(alog_ref[...]) * LOG2E
    push_chunks(b_ref, drive_ref, push_ref)

    def chunk(index, state):
        base = chunk_place(index, me, size)
        steps = delta_ref[pl.ds(base, CHUNK), :]
        for j in range(CHUNK):
            at = pl.ds(pl.multiple_of((base + j) * STATE, STATE), STATE)
            state = jnp.exp2(steps[j : j + 1, :] * rate) * state + push_ref[at, :]
            states_ref[at, :] = state.astype(bf16)
        return state

    lax.fori_loop(0, LEN // CHUNK, chunk, jnp.zeros((STATE, lanes), f32))

    def output(index, carry):
        for rows, many in chunk_group(index):
            ys_ref[rows, :] = matmul(c_ref[rows, :], states_ref[many, :])
        return carry

    lax.fori_loop(0, LEN // CHUNK // GROUP, output, 0)
    ys = ys_ref[...] + skip_ref[...] * u_ref[...]
    ys_ref[...] = ys
    zs = xz_ref[0]
    gated = (ys * (zs * sigmoid(zs))).astype(bf16)
    gated_ref[...] = gated
    part = matmul(gated, out_w_ref[...])

    @pl.when(step == 0)
    def _():
        total_ref[...] = part

    @pl.when(step > 0)
    def _():
        total_ref[...] += part

    @pl.when(step == pl.num_programs(0) - 1)
    def _():
        store_blocks(out_refs, total_ref[...])


def scan_backward_kernel(
    blocks,
    me_ref,
    proj_ref,
    dt_proj_ref,
    bias_ref,
    alog_ref,
    skip_ref,
    u_ref,
    xz_ref,
    out_w_ref,
    ys_ref,
    states_ref,
    *rest,
):
    grad_refs = rest[:blocks]
    (
        du_ref,
        dzs_ref,
        small_ref,
        dalog_ref,
        ddt_ref,
        dcols_ref,
        grad_ref,
        cols_ref,
        b_ref,
        c_ref,
        pb_ref,
        pc_ref,
        delta_ref,
        drive_ref,
        dys_ref,
        ddrive_ref,
        drate_ref,
        dlow_ref,
        push_ref,
        grads_ref,
        rates_ref,
    ) = rest[blocks:]
    me = me_ref[0]
    size = LEN // blocks
    lanes = u_ref.shape[1]
    step = pl.program_id(0)

    @pl.when(step == 0)
    def _():
        scan_setup(proj_ref, cols_ref, b_ref, c_ref)
        join_blocks(grad_refs, grad_ref)
        pb_ref[...] = jnp.zeros(pb_ref.shape, f32)
        pc_ref[...] = jnp.zeros(pc_ref.shape, f32)

    low, pre, delta = step_sizes(cols_ref, dt_proj_ref, bias_ref)
    u = u_ref[...]
    delta_ref[...] = delta
    drive_ref[...] = (delta * u).astype(bf16)
    dgated = times_transposed(grad_ref[...], out_w_ref[...])
    zs = xz_ref[0]
    gate = sigmoid(zs)
    dys = dgated * (zs * gate)
    dys_ref[...] = dys.astype(bf16)
    dzs_ref[...] = (dgated * ys_ref[...] * (gate * (1.0 + zs * (1.0 - gate)))).astype(bf16)
    a_matrix = -jnp.exp(alog_ref[...])
    rate = a_matrix * LOG2E
    chunks = LEN // CHUNK
    mask = chunk_mask(CHUNK)
    push_chunks(c_ref, dys_ref, push_ref)

    def chunk(step_index, carry):
        adjoint, da = carry
        index = chunks - 1 - step_index
        base = chunk_place(index, me, size)
        before = chunk_place(jnp.maximum(index - 1, 0), me, size)
        first = (index > 0).astype(f32)
        steps = delta_ref[pl.ds(base, CHUNK), :]
        for j in range(CHUNK - 1, -1, -1):
            at = pl.ds(pl.multiple_of((base + j) * STATE, STATE), STATE)
            if j > 0:
                last = (base + j - 1) * STATE
                earlier = states_ref[pl.ds(pl.multiple_of(last, STATE), STATE), :].astype(f32)
            else:
                last = (before + CHUNK - 1) * STATE
                earlier = states_ref[pl.ds(pl.multiple_of(last, STATE), STATE), :].astype(f32) * first
            grad = adjoint + push_ref[at, :]
            grads_ref[at, :] = grad.astype(bf16)
            adjoint = grad * jnp.exp2(steps[j : j + 1, :] * rate)
            through = adjoint * earlier
            rates_ref[at, :] = (through * a_matrix).astype(bf16)
            da = da + through * steps[j : j + 1, :]
        return adjoint, da

    zero = jnp.zeros((STATE, lanes), f32)
    _, da = lax.fori_loop(0, chunks, chunk, (zero, zero))
    mask_low = mask.astype(bf16)

    def output(index, carry):
        for rows, many in chunk_group(index):
            grads = grads_ref[many, :]
            ddrive_ref[rows, :] = matmul(b_ref[rows, :], grads)
            drate_ref[rows, :] = matmul(mask_low, rates_ref[many, :])
            pb_ref[rows, :] += times_transposed(drive_ref[rows, :], grads) * mask
            pc_ref[rows, :] += times_transposed(dys_ref[rows, :], states_ref[many, :]) * mask
        return carry

    lax.fori_loop(0, chunks // GROUP, output, 0)
    dalog_ref[...] = da * a_matrix
    ddrive = ddrive_ref[...]
    du_ref[...] = ddrive * delta + skip_ref[...] * dys
    dpre = (ddrive * u + drate_ref[...]) * sigmoid(pre)
    dpre_low = dpre.astype(bf16)
    small_ref[...] = jnp.concatenate(
        [
            jnp.sum(dpre, axis=0, keepdims=True),
            jnp.sum(dys * u, axis=0, keepdims=True),
            jnp.zeros((6, lanes), f32),
        ],
        axis=0,
    )
    ddt_ref[...] = transposed_times(low, dpre_low)
    part = times_transposed(dpre_low, dt_proj_ref[...])

    @pl.when(step == 0)
    def _():
        dlow_ref[...] = part

    @pl.when(step > 0)
    def _():
        dlow_ref[...] += part

    @pl.when(step == pl.num_programs(0) - 1)
    def _():
        collect = (
            lax.broadcasted_iota(jnp.int32, (CHUNK * STATE, STATE), 0) % STATE
            == lax.broadcasted_iota(jnp.int32, (CHUNK * STATE, STATE), 1)
        ).astype(f32)
        dcols_ref[...] = jnp.concatenate(
            [dlow_ref[...], dot_exact(pb_ref[...], collect), dot_exact(pc_ref[...], collect)], axis=1
        )


def conv_backward_kernel(
    blocks,
    me_ref,
    dcols_ref,
    proj_ref,
    u_ref,
    xz_ref,
    du_ref,
    weight_ref,
    xproj_ref,
    dxs_ref,
    dxproj_ref,
    dweight_ref,
    pad_ref,
    grad_ref,
):
    me = me_ref[0]
    size = LEN // blocks
    lanes = u_ref.shape[1]
    projected = proj_ref[...]
    scale, in_step, in_b, in_c, mean_b, mean_c = column_norm_parts(projected)
    normed = projected * scale
    dcols = dcols_ref[...]
    product = dcols * normed
    dot_step = jnp.sum(jnp.where(in_step, product, 0.0), axis=1, keepdims=True) / DT_RANK
    dot_b = jnp.sum(jnp.where(in_b, product, 0.0), axis=1, keepdims=True) / STATE
    dot_c = jnp.sum(jnp.where(in_c, product, 0.0), axis=1, keepdims=True) / STATE
    dot_b = jnp.where(mean_b > floor_square, dot_b, 0.0)
    dot_c = jnp.where(mean_c > floor_square, dot_c, 0.0)
    mean = jnp.where(in_step, dot_step, jnp.where(in_b, dot_b, dot_c))
    dproj = (scale * (dcols - normed * mean)).astype(bf16)
    dxproj_ref[...] = transposed_times(dproj, u_ref[...].astype(bf16))
    du = du_ref[...] + times_transposed(dproj, xproj_ref[...])
    pad_ref[0:PAD, :] = jnp.zeros((PAD, lanes), f32)
    grad_ref[LEN : LEN + PAD, :] = jnp.zeros((PAD, lanes), f32)
    for m in range(blocks):
        at = pl.multiple_of(jnp.bitwise_xor(me, m) * size, size)
        pad_ref[PAD + m * size : PAD + (m + 1) * size, :] = xz_ref[0, pl.ds(at, size), :]
    dxs_ref[...] = du.astype(bf16)
    du_ref_rows = []
    grad_ref[0:LEN, :] = du
    total = conv_total(pad_ref, weight_ref, LEN)
    gate = sigmoid(total)
    slope = gate * (1.0 + total * (1.0 - gate))
    for m in range(blocks):
        at = pl.multiple_of(jnp.bitwise_xor(me, m) * size, size)
        du_ref_rows.append(grad_ref[pl.ds(at, size), :])
    grad_ref[0:LEN, :] = jnp.concatenate(du_ref_rows, axis=0) * slope
    dcv = grad_ref[0:LEN, :]
    dweight_ref[...] = jnp.concatenate(
        [
            jnp.sum(dcv * pad_ref[pl.ds(PAD - CONV + 1 + tap, LEN), :], axis=0, keepdims=True)
            for tap in range(CONV)
        ],
        axis=0,
    )
    dxs = weight_ref[CONV - 1 : CONV, :] * dcv
    for tap in range(CONV - 1):
        dxs = dxs + weight_ref[tap : tap + 1, :] * grad_ref[pl.ds(CONV - 1 - tap, LEN), :]
    dxs = dxs.astype(bf16)
    for m in range(blocks):
        at = pl.multiple_of(jnp.bitwise_xor(me, m) * size, size)
        dxs_ref[pl.ds(at, size), :] = dxs[m * size : (m + 1) * size, :]


def store_blocks(refs, value):
    size = value.shape[0] // len(refs)
    for k, ref in enumerate(refs):
        ref[...] = value[k * size : (k + 1) * size].astype(ref.dtype)


def join_blocks(refs, out_ref):
    size = out_ref.shape[0] // len(refs)
    for k, ref in enumerate(refs):
        out_ref[k * size : (k + 1) * size, :] = ref[...]


SMEM = pl.BlockSpec(memory_space=pltpu.SMEM)


def whole(shape):
    return pl.BlockSpec(shape, lambda *_: (0,) * len(shape))


def params():
    return pltpu.CompilerParams(vmem_limit_bytes=VMEM_LIMIT)


def takes(microseconds):
    return pl.CostEstimate(
        flops=int(microseconds * 1.15e9), bytes_accessed=1 << 20, transcendentals=0
    )


def shape_of(shape, dtype=f32):
    return jax.ShapeDtypeStruct(shape, dtype)


def conv_forward(me, blocks, xz, weight, x_proj):
    channels = xz.shape[2]
    return pl.pallas_call(
        functools.partial(conv_forward_kernel, blocks),
        grid=(1,),
        in_specs=[
            SMEM,
            pl.BlockSpec((1, LEN, channels), lambda i: (0, 0, 0)),
            whole(weight.shape),
            whole(x_proj.shape),
        ],
        out_specs=(whole((LEN, channels)), whole((LEN, 128))),
        out_shape=(shape_of((LEN, channels)), shape_of((LEN, 128))),
        scratch_shapes=[pltpu.VMEM((LEN + PAD, channels), f32)],
        compiler_params=params(),
        cost_estimate=takes(3),
        name="conv_forward",
    )(me, xz, weight, x_proj)


def lane_block(channels):
    return channels


def scan_forward(me, blocks, proj, dt_proj, bias, alog, skip, u, xz, out_w):
    channels = u.shape[1]
    lanes = lane_block(channels)
    col = lambda i: (0, i)
    return pl.pallas_call(
        functools.partial(scan_forward_kernel, blocks),
        grid=(channels // lanes,),
        in_specs=[
            SMEM,
            whole((LEN, 128)),
            pl.BlockSpec((DT_RANK, lanes), col),
            pl.BlockSpec((1, lanes), col),
            pl.BlockSpec((STATE, lanes), col),
            pl.BlockSpec((1, lanes), col),
            pl.BlockSpec((LEN, lanes), col),
            pl.BlockSpec((1, LEN, lanes), lambda i: (1, 0, i)),
            pl.BlockSpec((lanes, D), lambda i: (i, 0)),
        ],
        out_specs=(
            pl.BlockSpec((LEN, lanes), col),
            pl.BlockSpec((LEN, lanes), col),
            pl.BlockSpec((LEN * STATE, lanes), col),
        )
        + (whole((LEN // blocks, D)),) * blocks,
        out_shape=(
            shape_of((LEN, channels), bf16),
            shape_of((LEN, channels)),
            shape_of((LEN * STATE, channels), bf16),
        )
        + (shape_of((LEN // blocks, D), bf16),) * blocks,
        scratch_shapes=[
            pltpu.VMEM((LEN, 128), f32),
            pltpu.VMEM((LEN, CHUNK * STATE), bf16),
            pltpu.VMEM((LEN, CHUNK * STATE), bf16),
            pltpu.VMEM((LEN, lanes), f32),
            pltpu.VMEM((LEN, lanes), bf16),
            pltpu.VMEM((LEN * STATE, lanes), f32),
            pltpu.VMEM((LEN, D), f32),
        ],
        compiler_params=params(),
        cost_estimate=takes(13),
        name="scan_forward",
    )(me, proj, dt_proj, bias, alog, skip, u, xz, out_w)


def scan_backward(me, blocks, proj, dt_proj, bias, alog, skip, u, xz, out_w, grad, ys, states):
    channels = u.shape[1]
    lanes = lane_block(channels)
    col = lambda i: (0, i)
    rows = pl.BlockSpec((LEN, lanes), col)
    return pl.pallas_call(
        functools.partial(scan_backward_kernel, blocks),
        grid=(channels // lanes,),
        in_specs=[
            SMEM,
            whole((LEN, 128)),
            pl.BlockSpec((DT_RANK, lanes), col),
            pl.BlockSpec((1, lanes), col),
            pl.BlockSpec((STATE, lanes), col),
            pl.BlockSpec((1, lanes), col),
            rows,
            pl.BlockSpec((1, LEN, lanes), lambda i: (1, 0, i)),
            pl.BlockSpec((lanes, D), lambda i: (i, 0)),
            rows,
            pl.BlockSpec((LEN * STATE, lanes), col),
        ]
        + [whole((LEN // blocks, D))] * blocks,
        out_specs=(
            rows,
            rows,
            pl.BlockSpec((8, lanes), col),
            pl.BlockSpec((STATE, lanes), col),
            pl.BlockSpec((DT_RANK, lanes), col),
            whole((LEN, 128)),
        ),
        out_shape=(
            shape_of((LEN, channels)),
            shape_of((LEN, channels), bf16),
            shape_of((8, channels)),
            shape_of((STATE, channels)),
            shape_of((DT_RANK, channels)),
            shape_of((LEN, 128)),
        ),
        scratch_shapes=[
            pltpu.VMEM((LEN, D), bf16),
            pltpu.VMEM((LEN, 128), f32),
            pltpu.VMEM((LEN, CHUNK * STATE), bf16),
            pltpu.VMEM((LEN, CHUNK * STATE), bf16),
            pltpu.VMEM((LEN, CHUNK * STATE), f32),
            pltpu.VMEM((LEN, CHUNK * STATE), f32),
            pltpu.VMEM((LEN, lanes), f32),
            pltpu.VMEM((LEN, lanes), bf16),
            pltpu.VMEM((LEN, lanes), bf16),
            pltpu.VMEM((LEN, lanes), f32),
            pltpu.VMEM((LEN, lanes), f32),
            pltpu.VMEM((LEN, DT_RANK), f32),
            pltpu.VMEM((LEN * STATE, lanes), f32),
            pltpu.VMEM((LEN * STATE, lanes), bf16),
            pltpu.VMEM((LEN * STATE, lanes), bf16),
        ],
        compiler_params=params(),
        cost_estimate=takes(21),
        name="scan_backward",
    )(me, proj, dt_proj, bias, alog, skip, u, xz, out_w, ys, states, *grad)


def conv_backward(me, blocks, dcols, proj, u, xz, du, weight, x_proj):
    channels = u.shape[1]
    return pl.pallas_call(
        functools.partial(conv_backward_kernel, blocks),
        grid=(1,),
        in_specs=[
            SMEM,
            whole((LEN, 128)),
            whole((LEN, 128)),
            whole((LEN, channels)),
            pl.BlockSpec((1, LEN, channels), lambda i: (0, 0, 0)),
            whole((LEN, channels)),
            whole(weight.shape),
            whole(x_proj.shape),
        ],
        out_specs=(whole((LEN, channels)), whole((128, channels)), whole((CONV, channels))),
        out_shape=(
            shape_of((LEN, channels), bf16),
            shape_of((128, channels)),
            shape_of((CONV, channels)),
        ),
        scratch_shapes=[
            pltpu.VMEM((LEN + PAD, channels), f32),
            pltpu.VMEM((LEN + PAD, channels), f32),
        ],
        compiler_params=params(),
        cost_estimate=takes(5),
        name="conv_backward",
    )(me, dcols, proj, u, xz, du, weight, x_proj)


def attention_probabilities(q, k, allowed):
    scores = times_transposed(q, k) * (1.0 / math.sqrt(HEAD_DIM))
    scores = jnp.where(allowed, scores, masked_score)
    peak = jnp.max(scores, axis=1, keepdims=True)
    exponent = jnp.exp(scores - peak)
    return exponent / jnp.sum(exponent, axis=1, keepdims=True)


def causal(me, blocks):
    size = LEN // blocks

    def position(axis):
        index = lax.broadcasted_iota(jnp.int32, (LEN, LEN), axis)
        return jnp.bitwise_xor(index // size, me) * size + index % size

    return position(1) <= position(0)


def attention_forward_kernel(
    blocks, me_ref, wq_ref, wkv_ref, wo_ref, *rest
):
    joined_ref, q_ref, kv_ref, o_ref = rest[blocks : blocks + 4]
    out_refs = rest[blocks + 4 :]
    join_blocks(rest[:blocks], joined_ref)
    normed = joined_ref[...]
    q_ref[...] = matmul(normed, wq_ref[...]).astype(bf16)
    kv_ref[...] = matmul(normed, wkv_ref[...]).astype(bf16)
    kv_heads = wkv_ref.shape[1] // (2 * HEAD_DIM)
    group = HEADS // KV_HEADS
    allowed = causal(me_ref[0], blocks)
    outs = []
    for head in range(kv_heads * group):
        kv = head // group
        q = q_ref[:, head * HEAD_DIM : (head + 1) * HEAD_DIM]
        k = kv_ref[:, kv * HEAD_DIM : (kv + 1) * HEAD_DIM]
        v = kv_ref[:, (kv_heads + kv) * HEAD_DIM : (kv_heads + kv + 1) * HEAD_DIM]
        soft = attention_probabilities(q, k, allowed)
        outs.append(matmul(soft.astype(bf16), v).astype(bf16))
    o_ref[...] = jnp.concatenate(outs, axis=1)
    store_blocks(out_refs, matmul(o_ref[...], wo_ref[...]))


def attention_backward_kernel(
    blocks,
    me_ref,
    q_ref,
    kv_ref,
    wq_ref,
    wkv_ref,
    wo_ref,
    *rest,
):
    dqkv_ref, grad_ref = rest[blocks], rest[-1]
    join_blocks(rest[:blocks], grad_ref)
    dout = times_transposed(grad_ref[...], wo_ref[...]).astype(bf16)
    kv_heads = wkv_ref.shape[1] // (2 * HEAD_DIM)
    group = HEADS // KV_HEADS
    allowed = causal(me_ref[0], blocks)
    scale = 1.0 / math.sqrt(HEAD_DIM)
    dqs, dks, dvs = [], [], []
    for kv in range(kv_heads):
        k = kv_ref[:, kv * HEAD_DIM : (kv + 1) * HEAD_DIM]
        v = kv_ref[:, (kv_heads + kv) * HEAD_DIM : (kv_heads + kv + 1) * HEAD_DIM]
        dk = jnp.zeros((LEN, HEAD_DIM), f32)
        dv = jnp.zeros((LEN, HEAD_DIM), f32)
        for head in range(kv * group, (kv + 1) * group):
            q = q_ref[:, head * HEAD_DIM : (head + 1) * HEAD_DIM]
            do = dout[:, head * HEAD_DIM : (head + 1) * HEAD_DIM]
            soft = attention_probabilities(q, k, allowed)
            dsoft = times_transposed(do, v)
            dscore = soft * (dsoft - jnp.sum(soft * dsoft, axis=1, keepdims=True))
            dscore = dscore.astype(bf16)
            dqs.append((matmul(dscore, k) * scale).astype(bf16))
            dk = dk + transposed_times(dscore, q) * scale
            dv = dv + transposed_times(soft.astype(bf16), do)
        dks.append(dk.astype(bf16))
        dvs.append(dv.astype(bf16))
    dq = jnp.concatenate(dqs, axis=1)
    dkv = jnp.concatenate(dks + dvs, axis=1)
    dqkv_ref[:, : dq.shape[1]] = dq
    dqkv_ref[:, dq.shape[1] :] = dkv
    dn = times_transposed(dq, wq_ref[...]) + times_transposed(dkv, wkv_ref[...])
    store_blocks(rest[blocks + 1 : -1], dn)


def attention_forward(me, blocks, normed, wq, wkv, wo):
    size = LEN // blocks
    heads = shape_of((LEN, wq.shape[1]), bf16)
    kept = (shape_of((LEN, D), bf16), heads, shape_of((LEN, wkv.shape[1]), bf16), heads)
    return pl.pallas_call(
        functools.partial(attention_forward_kernel, blocks),
        grid=(1,),
        in_specs=[SMEM, whole(wq.shape), whole(wkv.shape), whole(wo.shape)]
        + [whole((size, D))] * blocks,
        out_specs=tuple(whole(item.shape) for item in kept) + (whole((size, D)),) * blocks,
        out_shape=kept + (shape_of((size, D), bf16),) * blocks,
        compiler_params=params(),
        cost_estimate=takes(6),
        name="attention_forward",
    )(me, wq, wkv, wo, *normed)


def attention_backward(me, blocks, grad, q, kv, wq, wkv, wo):
    size = LEN // blocks
    cols = wq.shape[1] + wkv.shape[1]
    return pl.pallas_call(
        functools.partial(attention_backward_kernel, blocks),
        grid=(1,),
        in_specs=[
            SMEM,
            whole(q.shape),
            whole(kv.shape),
            whole(wq.shape),
            whole(wkv.shape),
            whole(wo.shape),
        ]
        + [whole((size, D))] * blocks,
        out_specs=(whole((LEN, cols)),) + (whole((size, D)),) * blocks,
        out_shape=(shape_of((LEN, cols), bf16),) + (shape_of((size, D), bf16),) * blocks,
        scratch_shapes=[pltpu.VMEM((LEN, D), bf16)],
        compiler_params=params(),
        cost_estimate=takes(8),
        name="attention_backward",
    )(me, q, kv, wq, wkv, wo, *grad)


def norm_forward_kernel(hidden_ref, gain_ref, *rest):
    part_refs, (out_ref, normed_ref) = rest[:-2], rest[-2:]
    hidden = hidden_ref[...]
    for ref in part_refs:
        hidden = hidden + ref[...].astype(f32)
    scale = lax.rsqrt(jnp.mean(hidden * hidden, axis=1, keepdims=True) + epsilon)
    out_ref[...] = hidden
    normed_ref[...] = (hidden * scale * gain_ref[...]).astype(bf16)


def norm_forward(hidden, gain, parts):
    shape = hidden.shape
    return pl.pallas_call(
        norm_forward_kernel,
        grid=(1,),
        in_specs=[whole(shape), whole((1, D))] + [whole(shape)] * len(parts),
        out_specs=(whole(shape), whole(shape)),
        out_shape=(shape_of(shape), shape_of(shape, bf16)),
        compiler_params=params(),
        cost_estimate=takes(2),
        name="norm_forward",
    )(hidden, gain, *parts)


def pull_norm(grad, hidden, gain):
    scale = lax.rsqrt(jnp.mean(hidden * hidden, axis=1, keepdims=True) + epsilon)
    unit = hidden * scale
    through = grad * gain
    back = scale * (through - unit * jnp.mean(through * unit, axis=1, keepdims=True))
    return back, jnp.sum(grad * unit, axis=0, keepdims=True)


def norm_backward_kernel(grad_ref, hidden_ref, gain_ref, *rest):
    part_refs, (out_ref, low_ref, dgain_ref) = rest[:-3], rest[-3:]
    dn = part_refs[0][...].astype(f32)
    for ref in part_refs[1:]:
        dn = dn + ref[...].astype(f32)
    back, dgain = pull_norm(dn, hidden_ref[...], gain_ref[...])
    grad = grad_ref[...] + back
    out_ref[...] = grad
    low_ref[...] = grad.astype(bf16)
    dgain_ref[...] = dgain


def norm_backward(grad, hidden, gain, parts):
    shape = hidden.shape
    return pl.pallas_call(
        norm_backward_kernel,
        grid=(1,),
        in_specs=[whole(shape), whole(shape), whole((1, D))] + [whole(shape)] * len(parts),
        out_specs=(whole(shape), whole(shape), whole((1, D))),
        out_shape=(shape_of(shape), shape_of(shape, bf16), shape_of((1, D))),
        compiler_params=params(),
        cost_estimate=takes(2.5),
        name="norm_backward",
    )(grad, hidden, gain, *parts)


def router_backward_kernel(grad_ref, hidden_ref, gain_ref, normed_ref, picks_ref, router_ref, *rest):
    part_refs, (out_ref, low_ref, dgain_ref, drouter_ref) = rest[:-4], rest[-4:]
    dn = part_refs[0][...].astype(f32)
    for ref in part_refs[1:]:
        dn = dn + ref[...].astype(f32)
    normed, router = normed_ref[...], router_ref[...]
    rows = normed.shape[0]
    ids = lax.broadcasted_iota(jnp.int32, (rows, EXPERTS), 1)
    logits = times_transposed(normed, router)
    hot = [(ids == picks_ref[:, k : k + 1]).astype(f32) for k in (0, 1)]
    chosen = [jnp.sum(hot[k] * logits, axis=1, keepdims=True) for k in (0, 1)]
    peak = jnp.maximum(chosen[0], chosen[1])
    weight = [jnp.exp(value - peak) for value in chosen]
    total = weight[0] + weight[1]
    weight = [value / total for value in weight]
    dw = [dn[:, D + k : D + k + 1] for k in (0, 1)]
    mean = weight[0] * dw[0] + weight[1] * dw[1]
    dlog = sum(hot[k] * (weight[k] * (dw[k] - mean)) for k in (0, 1)).astype(bf16)
    dn = dn[:, :D] + matmul(dlog, router)
    back, dgain = pull_norm(dn, hidden_ref[...], gain_ref[...])
    grad = grad_ref[...].astype(f32) + back
    out_ref[...] = grad
    low_ref[...] = grad.astype(bf16)
    dgain_ref[...] = dgain
    drouter_ref[...] = transposed_times(dlog, normed)


def router_backward(grad, hidden, gain, normed, picks, router, parts):
    shape = hidden.shape
    wide_rows = whole((shape[0], D + 128))
    return pl.pallas_call(
        router_backward_kernel,
        grid=(1,),
        in_specs=[
            whole(shape),
            whole(shape),
            whole((1, D)),
            whole(shape),
            whole((shape[0], 2)),
            whole((EXPERTS, D)),
        ]
        + [wide_rows] * len(parts),
        out_specs=(whole(shape), whole(shape), whole((1, D)), whole((EXPERTS, D))),
        out_shape=(
            shape_of(shape),
            shape_of(shape, bf16),
            shape_of((1, D)),
            shape_of((EXPERTS, D)),
        ),
        compiler_params=params(),
        cost_estimate=takes(3),
        name="router_backward",
    )(grad, hidden, gain, normed, picks, router, *parts)


def experts_kernel(blocks, routes_ref, router_ref, w_in_ref, w_out_ref, *rest):
    normed_refs, grad_refs = rest[:blocks], rest[blocks : 2 * blocks]
    moved_ref, act_ref, weighted_ref = rest[2 * blocks : 2 * blocks + 3]
    dn_refs = rest[2 * blocks + 3 : 3 * blocks + 3]
    (
        normed_ref,
        grad_ref,
        even_ref,
        odd_ref,
        grads_ref,
        place_ref,
        first_ref,
        second_ref,
        scale_ref,
        back_ref,
        kept_ref,
        dw_ref,
    ) = rest[3 * blocks + 3 :]
    expert = pl.program_id(0)
    slots = EXPERTS * CAP
    units = w_out_ref.shape[1]

    @pl.when(expert == 0)
    def _():
        join_blocks(normed_refs, normed_ref)
        join_blocks(grad_refs, grad_ref)
        routes = routes_ref[...]
        ids = lax.broadcasted_iota(jnp.int32, (EXPERTS, LEN), 0)
        hot = [(ids == routes[k : k + 1, :]).astype(f32) for k in (0, 1)]
        earlier = (
            lax.broadcasted_iota(jnp.int32, (LEN, LEN), 0)
            < lax.broadcasted_iota(jnp.int32, (LEN, LEN), 1)
        ).astype(bf16)
        rank0 = matmul(hot[0].astype(bf16), earlier)
        rank1 = matmul(hot[1].astype(bf16), earlier) + jnp.sum(hot[0], axis=1, keepdims=True)
        first = ids.astype(f32) * CAP
        position = [
            jnp.sum(hot[k] * (first + rank), axis=0, keepdims=True).astype(jnp.int32)
            for k, rank in ((0, rank0), (1, rank1))
        ]
        logits = times_transposed(router_ref[...], normed_ref[...])
        chosen = [jnp.sum(hot[k] * logits, axis=0, keepdims=True) for k in (0, 1)]
        peak = jnp.maximum(chosen[0], chosen[1])
        weight = [jnp.exp(value - peak) for value in chosen]
        total = weight[0] + weight[1]
        weight = [value / total for value in weight]
        slot = lax.broadcasted_iota(jnp.int32, (slots, LEN), 0)
        in0 = (slot == position[0]).astype(f32)
        in1 = (slot == position[1]).astype(f32)
        weighted = in0 * weight[0] + in1 * weight[1]
        place = (in0 + in1).astype(bf16)
        first_ref[...] = in0.astype(bf16)
        second_ref[...] = in1.astype(bf16)
        place_ref[...] = place
        weighted_ref[...] = weighted.astype(bf16)
        scale_ref[...] = jnp.broadcast_to(jnp.sum(weighted, axis=1, keepdims=True), (slots, 128))
        grads_ref[...] = matmul(place, grad_ref[...]).astype(bf16)
        spread = lax.broadcasted_iota(jnp.int32, (128, 256), 1) - 2 * lax.broadcasted_iota(
            jnp.int32, (128, 256), 0
        )
        for block in range(D // 128):
            rows = matmul(place, normed_ref[:, block * 128 : (block + 1) * 128]).astype(bf16)
            cols = slice(block * 256, (block + 1) * 256)
            even_ref[:, cols] = matmul(rows, (spread == 0).astype(bf16)).astype(bf16)
            odd_ref[:, cols] = matmul(rows, (spread == 1).astype(bf16)).astype(bf16)

    mine = pl.ds(pl.multiple_of(expert * CAP, CAP), CAP)
    w_in = w_in_ref[0].reshape(2 * D, units)
    w_out = w_out_ref[0]
    both = matmul(jnp.concatenate([even_ref[mine, :], odd_ref[mine, :]], axis=0), w_in)
    gate, up = both[:CAP], both[CAP:]
    sig = sigmoid(gate)
    silu = gate * sig
    act = silu * up
    act_low = act.astype(bf16)
    act_ref[0] = act_low
    scale = scale_ref[mine, 0:1]
    plain = times_transposed(grads_ref[mine, :], w_out)
    dw_ref[mine, :] = jnp.broadcast_to(
        jnp.sum(plain * act_low.astype(f32), axis=1, keepdims=True), (CAP, 128)
    ).astype(bf16)
    dact = plain * scale
    dgate = (dact * sig * (1.0 + gate * (1.0 - sig)) * up).astype(bf16)
    dup = (dact * silu).astype(bf16)
    back = times_transposed(jnp.concatenate([dgate, dup], axis=0), w_in)
    lane = lax.broadcasted_iota(jnp.int32, (CAP, 2 * D), 1)
    back_ref[mine, :] = jnp.where(lane % 2 == 0, back[:CAP], back[CAP:]).astype(bf16)
    kept_ref[mine, :] = jnp.concatenate([dgate, dup, (act * scale).astype(bf16)], axis=1)

    @pl.when(expert == EXPERTS - 1)
    def _():
        pairs = (
            lax.broadcasted_iota(jnp.int32, (256, 128), 0) // 2
            == lax.broadcasted_iota(jnp.int32, (256, 128), 1)
        ).astype(bf16)
        size = LEN // blocks
        for block in range(D // 128):
            cols = slice(block * 256, (block + 1) * 256)
            wide_rows = transposed_times(place_ref[...], back_ref[:, cols]).astype(bf16)
            dn = matmul(wide_rows, pairs).astype(bf16)
            for k, ref in enumerate(dn_refs):
                ref[:, block * 128 : (block + 1) * 128] = dn[k * size : (k + 1) * size]
        lanes = lax.broadcasted_iota(jnp.int32, (LEN, 128), 1)
        gates = [transposed_times(ref[...], dw_ref[...]) for ref in (first_ref, second_ref)]
        gates = jnp.where(lanes == 0, gates[0], jnp.where(lanes == 1, gates[1], 0.0)).astype(bf16)
        for k, ref in enumerate(dn_refs):
            ref[:, D:] = gates[k * size : (k + 1) * size]
        for k, ref in enumerate((first_ref, second_ref)):
            moved_ref[:, k * 3 * units : (k + 1) * 3 * units] = transposed_times(
                ref[...], kept_ref[...]
            ).astype(bf16)


def experts(blocks, routes, router, normed, grad, w_in, w_out):
    units = w_out.shape[1]
    slots = EXPERTS * CAP
    size = LEN // blocks
    return pl.pallas_call(
        functools.partial(experts_kernel, blocks),
        grid=(EXPERTS,),
        in_specs=[
            whole((2, LEN)),
            whole((EXPERTS, D)),
            pl.BlockSpec((1, D, 2, units), lambda e: (e, 0, 0, 0)),
            pl.BlockSpec((1, units, D), lambda e: (e, 0, 0)),
        ]
        + [whole((size, D))] * (2 * blocks),
        out_specs=(
            whole((LEN, 6 * units)),
            pl.BlockSpec((1, CAP, units), lambda e: (e, 0, 0)),
            whole((slots, LEN)),
        )
        + (whole((size, D + 128)),) * blocks,
        out_shape=(
            shape_of((LEN, 6 * units), bf16),
            shape_of((EXPERTS, CAP, units), bf16),
            shape_of((slots, LEN), bf16),
        )
        + (shape_of((size, D + 128), bf16),) * blocks,
        scratch_shapes=[
            pltpu.VMEM((LEN, D), bf16),
            pltpu.VMEM((LEN, D), bf16),
            pltpu.VMEM((slots, 2 * D), bf16),
            pltpu.VMEM((slots, 2 * D), bf16),
            pltpu.VMEM((slots, D), bf16),
            pltpu.VMEM((slots, LEN), bf16),
            pltpu.VMEM((slots, LEN), bf16),
            pltpu.VMEM((slots, LEN), bf16),
            pltpu.VMEM((slots, 128), f32),
            pltpu.VMEM((slots, 2 * D), bf16),
            pltpu.VMEM((slots, 3 * units), bf16),
            pltpu.VMEM((slots, 128), bf16),
        ],
        compiler_params=params(),
        cost_estimate=takes(37),
        name="experts",
    )(routes, router, w_in, w_out, *normed, *grad)


def experts_out_kernel(act_ref, weighted_ref, w_out_ref, *rest):
    made_refs, ye_ref = rest[:-1], rest[-1]
    expert = pl.program_id(0)
    mine = pl.ds(pl.multiple_of(expert * CAP, CAP), CAP)
    ye_ref[mine, :] = matmul(act_ref[0], w_out_ref[0]).astype(bf16)

    @pl.when(expert == EXPERTS - 1)
    def _():
        store_blocks(made_refs, transposed_times(weighted_ref[...], ye_ref[...]))


def experts_out(blocks, act, weighted, w_out):
    units = w_out.shape[1]
    slots = EXPERTS * CAP
    return pl.pallas_call(
        experts_out_kernel,
        grid=(EXPERTS,),
        in_specs=[
            pl.BlockSpec((1, CAP, units), lambda e: (e, 0, 0)),
            whole((slots, LEN)),
            pl.BlockSpec((1, units, D), lambda e: (e, 0, 0)),
        ],
        out_specs=(whole((LEN // blocks, D)),) * blocks,
        out_shape=(shape_of((LEN // blocks, D), bf16),) * blocks,
        scratch_shapes=[pltpu.VMEM((slots, D), bf16)],
        compiler_params=params(),
        cost_estimate=takes(14),
        name="experts_out",
    )(act, weighted, w_out)


def sort_rows(refs, groups, out_ref):
    share = LEN // len(refs)
    for group in range(groups):
        for k, ref in enumerate(refs):
            at = group * LEN + k * share
            out_ref[at : at + share, :] = ref[group * share : (group + 1) * share, :]


def sorted_columns_kernel(groups, *refs):
    column_refs, (left_ref, right_ref, picks_ref, rows_ref) = refs[:-4], refs[-4:]
    width = left_ref.shape[0]
    sort_rows(column_refs, groups, rows_ref)
    left_ref[...] = rows_ref[:, :width].astype(f32).T.astype(bf16)
    right_ref[...] = rows_ref[:, width : 2 * width].astype(f32).T.astype(bf16)
    picks_ref[...] = rows_ref[:, 4 * width : 4 * width + 2].astype(f32)


def sorted_columns(groups, columns):
    tokens, width = groups * LEN, D // groups
    shapes = ((width, tokens), (width, tokens))
    return pl.pallas_call(
        functools.partial(sorted_columns_kernel, groups),
        grid=(1,),
        in_specs=[whole(item.shape) for item in columns],
        out_specs=tuple(whole(shape) for shape in shapes) + (whole((tokens, 2)),),
        out_shape=tuple(shape_of(shape, bf16) for shape in shapes) + (shape_of((tokens, 2)),),
        scratch_shapes=[pltpu.VMEM((tokens, columns[0].shape[1]), bf16)],
        compiler_params=params(),
        cost_estimate=takes(4),
        name="sorted_columns",
    )(*columns)


def expert_grad_kernel(first, moved_ref, left_ref, right_ref, picks_ref, *rest):
    din_ref, dout_ref = rest[-2:]
    units = moved_ref.shape[1] // 6
    which = (pl.program_id(0) + first).astype(f32)
    at0 = (picks_ref[:, 0:1] == which).astype(bf16)
    at1 = (picks_ref[:, 1:2] == which).astype(bf16)
    moved = moved_ref[:, : 3 * units] * at0 + moved_ref[:, 3 * units :] * at1
    din = matmul(left_ref[...], moved[:, : 2 * units])
    din_ref[0, :, 0, :] = din[:, :units]
    din_ref[0, :, 1, :] = din[:, units:]
    dout_ref[0] = matmul(right_ref[...], moved[:, 2 * units :])


def expert_grads(first, count, moved, left, right, picks, earlier=()):
    width = left.shape[0]
    units = moved.shape[1] // 6
    inputs = (moved, left, right, picks)
    return pl.pallas_call(
        functools.partial(expert_grad_kernel, first),
        grid=(count,),
        in_specs=[whole(item.shape) for item in inputs]
        + [pl.BlockSpec(memory_space=pl.ANY)] * len(earlier),
        out_specs=(
            pl.BlockSpec((1, width, 2, units), lambda e: (e + first, 0, 0, 0)),
            pl.BlockSpec((1, width, units), lambda e: (e + first, 0, 0)),
        ),
        out_shape=(
            shape_of((EXPERTS, width, 2, units)),
            shape_of((EXPERTS, width, units)),
        ),
        input_output_aliases={4: 0, 5: 1} if earlier else {},
        compiler_params=params(),
        cost_estimate=takes(1.5 * count),
        name="expert_grads",
    )(*inputs, *earlier)


def pack_columns_kernel(groups, lanes, *refs):
    in_refs, out_ref = refs[:-1], refs[-1]
    width = D // groups
    values = [ref[...].astype(f32) for ref in in_refs]
    rows = values[0].shape[0]
    for group in range(groups):
        parts = [
            value[:, group * width : (group + 1) * width] if value.shape[1] == D else value
            for value in values
        ]
        spare = lanes - sum(part.shape[1] for part in parts)
        if spare:
            parts.append(jnp.zeros((rows, spare), f32))
        whole_row = jnp.concatenate(parts, axis=1) if len(parts) > 1 else parts[0]
        out_ref[group] = whole_row.astype(bf16)


def pack_columns(groups, *values):
    width, rows = D // groups, values[0].shape[0]
    lanes = sum(width if value.shape[1] == D else value.shape[1] for value in values)
    if len(values) > 1:
        lanes += -lanes % 128
    return pl.pallas_call(
        functools.partial(pack_columns_kernel, groups, lanes),
        grid=(1,),
        in_specs=[whole(value.shape) for value in values],
        out_specs=whole((groups, rows, lanes)),
        out_shape=shape_of((groups, rows, lanes), bf16),
        compiler_params=params(),
        cost_estimate=takes(3),
        name="pack_columns",
    )(*values)


def mix_grad_kernel(groups, normed_ref, first_ref, second_ref, *refs):
    extra_refs, out_ref = refs[:-1], refs[-1]
    width = D // groups
    grads = [
        transposed_times(normed_ref[...], ref[...]).astype(bf16) for ref in (first_ref, second_ref)
    ]
    channels = grads[0].shape[1]
    share = channels // groups
    extras = [ref[...] for ref in extra_refs]
    for group in range(groups):
        at = 0
        for grad in grads:
            out_ref[group, at : at + width, :] = grad[group * width : (group + 1) * width]
            at += width
        for extra in extras:
            if extra.shape[0] > STATE:
                count = extra.shape[0] // groups
                part = extra[group * count : (group + 1) * count]
            else:
                count = extra.shape[0]
                part = extra[:, group * share : (group + 1) * share]
                part = jnp.concatenate([part, jnp.zeros((count, channels - share), f32)], axis=1)
            spare = -count % 16
            if spare:
                part = jnp.concatenate([part, jnp.zeros((spare, channels), f32)], axis=0)
            out_ref[group, at : at + count + spare, :] = part.astype(bf16)
            at += count + spare


def mix_grads(groups, normed, first, second, *extras):
    channels = first.shape[1]
    rows = 2 * (D // groups)
    for extra in extras:
        count = extra.shape[0] // groups if extra.shape[0] > STATE else extra.shape[0]
        rows += count + -count % 16
    return pl.pallas_call(
        functools.partial(mix_grad_kernel, groups),
        grid=(1,),
        in_specs=[whole(item.shape) for item in (normed, first, second) + extras],
        out_specs=whole((groups, rows, channels)),
        out_shape=shape_of((groups, rows, channels), bf16),
        compiler_params=params(),
        cost_estimate=takes(7),
        name="mix_grads",
    )(normed, first, second, *extras)


def out_grad_kernel(groups, first, heads_ref, acted_ref, *rest):
    column_refs, out_refs, rows_ref = rest[:-3], rest[-3:-1], rest[-1]
    width = out_refs[0].shape[0]
    sort_rows(column_refs, groups, rows_ref)
    for k, (left_ref, out_ref) in enumerate(zip((heads_ref, acted_ref), out_refs)):
        columns = rows_ref[:, (first + k) * width : (first + k + 1) * width]
        out_ref[...] = transposed_times(columns, left_ref[...])


def out_grads(groups, first, columns, heads, acted):
    width = D // groups
    lefts = (heads, acted)
    return pl.pallas_call(
        functools.partial(out_grad_kernel, groups, first),
        grid=(1,),
        in_specs=[whole(item.shape) for item in lefts + tuple(columns)],
        out_specs=tuple(whole((width, item.shape[1])) for item in lefts),
        out_shape=tuple(shape_of((width, item.shape[1])) for item in lefts),
        scratch_shapes=[pltpu.VMEM((groups * LEN, columns[0].shape[1]), bf16)],
        compiler_params=params(),
        cost_estimate=takes(6),
        name="out_grads",
    )(*lefts, *columns)


def last_grad_kernel(groups, gated_ref, *rest):
    column_refs, (out_ref, sums_ref, rows_ref) = rest[:-3], rest[-3:]
    share = LEN // len(column_refs)
    stride = column_refs[0].shape[0] // groups
    sums = jnp.zeros(sums_ref.shape, f32)
    for group in range(groups):
        for k, ref in enumerate(column_refs):
            at = group * LEN + k * share
            first = group * stride
            rows_ref[at : at + share, :] = ref[first : first + share, :]
            sums = sums + ref[first + share : first + stride, :].astype(f32)
    sums_ref[...] = sums
    out_ref[...] = transposed_times(rows_ref[...], gated_ref[...])


def last_grads(groups, columns, gated):
    width = D // groups
    extra = columns[0].shape[0] // groups - LEN // len(columns)
    shapes = ((width, gated.shape[1]), (extra, width))
    return pl.pallas_call(
        functools.partial(last_grad_kernel, groups),
        grid=(1,),
        in_specs=[whole(gated.shape)] + [whole(item.shape) for item in columns],
        out_specs=tuple(whole(shape) for shape in shapes),
        out_shape=tuple(shape_of(shape) for shape in shapes),
        scratch_shapes=[pltpu.VMEM((groups * LEN, width), bf16)],
        compiler_params=params(),
        cost_estimate=takes(5),
        name="last_grads",
    )(gated, *columns)


def shards(
    tokens,
    cotangent,
    norm_gains,
    mix_in,
    conv_weight,
    x_proj,
    dt_proj,
    dt_bias,
    a_log,
    skip_gain,
    mix_out,
    ffn_in,
    ffn_out,
    attn_query,
    attn_keyval,
    attn_out,
    router,
    expert_in,
    expert_out,
    routes,
):
    members = lax.axis_size("tensor")
    member = lax.axis_index("tensor")
    share = LEN // members
    groups = lax.axis_size("dp")
    gains = norm_gains.astype(f32)
    me = member.astype(jnp.int32).reshape(1)

    def swap(value, k):
        return lax.ppermute(value, "tensor", [(i, i ^ k) for i in range(members)])

    def join_list(rows):
        return [rows] + [swap(rows, k) for k in range(1, members)]

    def join(rows):
        return jnp.concatenate(join_list(rows), axis=0)

    def split_list(blocks):
        return [blocks[0]] + [swap(blocks[k], k) for k in range(1, members)]

    def blocks_of(partial):
        return [partial[k * share : (k + 1) * share].astype(bf16) for k in range(members)]

    def all_sum(partial):
        total = partial.astype(f32)
        for k in range(1, members):
            total = total + swap(partial, k).astype(f32)
        return total

    def all_sum_rows(partial):
        total = partial.astype(f32)
        for k in range(1, members):
            blocks = swap(partial, k).reshape(members, share, -1)
            ordered = jnp.concatenate([blocks[j ^ k] for j in range(members)], axis=0)
            total = total + ordered.astype(f32)
        return total

    def dp_scatter(value):
        return lax.psum_scatter(value, "dp", scatter_dimension=0, tiled=True)

    def dp_gather(value):
        return lax.all_gather(value, "dp", axis=0, tiled=True)

    def to_columns(*rows):
        came = lax.all_to_all(pack_columns(groups, *rows), "dp", 0, 0, tiled=True)
        return came.reshape(-1, came.shape[2])

    def hold(value, *others):
        return lax.optimization_barrier((value,) + others)[0]

    def gain(index):
        return gains[index : index + 1]

    hidden1, rows1 = norm_forward(tokens.astype(f32), gain(0), [])
    normed1 = join(rows1)
    channels = mix_in.shape[2]
    bias, skip = dt_bias.reshape(1, channels), skip_gain.reshape(1, channels)
    alog = a_log.T
    xz = jnp.einsum("td,dgc->gtc", normed1, mix_in, preferred_element_type=f32)
    u, proj_part = conv_forward(me, members, xz, conv_weight, x_proj)
    proj = all_sum_rows(proj_part)
    gated_low, ys, states, *mixed = scan_forward(
        me, members, proj, dt_proj, bias, alog, skip, u, xz, mix_out
    )
    all_gated = dp_gather(gated_low)
    hidden2, rows2 = norm_forward(hidden1, gain(1), split_list(mixed))
    normed2 = join(rows2)
    gate_up = jnp.einsum("td,dgc->gtc", normed2, ffn_in, preferred_element_type=f32)
    ffn_gate = sigmoid(gate_up[0])
    acted_low = (gate_up[0] * ffn_gate * gate_up[1]).astype(bf16)
    all_acted = dp_gather(acted_low)
    hidden3, rows3 = norm_forward(
        hidden2, gain(2), split_list(blocks_of(matmul(acted_low, ffn_out)))
    )
    keyval = attn_keyval.reshape(D, -1)
    rows3 = join_list(rows3)
    rows3[0] = hold(rows3[0], all_gated)
    normed3, query_low, keyval_low, attended_low, *attended = attention_forward(
        me, members, rows3, attn_query, keyval, attn_out
    )
    all_attended = dp_gather(attended_low)
    hidden4, rows4 = norm_forward(hidden3, gain(3), split_list(attended))
    normed4 = join_list(rows4)

    at = jnp.bitwise_xor(jnp.arange(members, dtype=jnp.int32), member)
    picks = routes.reshape(members, share, 2)[at].reshape(LEN, 2)
    own_picks = picks[:share]
    router_rows = router.T
    moved, expert_low, slot_weights, *dn_part = experts(
        members, picks.T, router_rows, normed4, join_list(cotangent), expert_in, expert_out
    )
    dn_part[0] = hold(dn_part[0], all_acted, all_attended)
    all_moved = dp_gather(moved)
    grad, low4, gain4, grad_router = router_backward(
        cotangent, hidden4, gain(3), rows4, own_picks, router_rows, split_list(dn_part)
    )
    grad_low4 = join_list(low4)

    width = D // groups
    units = expert_out.shape[1]

    dqkv, *dnormed = attention_backward(
        me, members, grad_low4, query_low, keyval_low, attn_query, keyval, attn_out
    )
    dn_blocks = split_list(dnormed)
    attn_in_part = transposed_times(normed3, dqkv).astype(bf16)
    attn_in_sum = dp_scatter(attn_in_part)
    grad, low3, gain3 = norm_backward(
        hold(grad, attn_in_part), hidden3, gain(2), dn_blocks
    )
    grad_low3 = join(low3)

    dact = times_transposed(grad_low3, ffn_out)
    dgate_up = jnp.concatenate(
        [
            dact * ffn_gate * (1.0 + gate_up[0] * (1.0 - ffn_gate)) * gate_up[1],
            dact * gate_up[0] * ffn_gate,
        ],
        axis=1,
    ).astype(bf16)
    hidden_units = ffn_in.shape[2]
    dnormed = jnp.einsum(
        "tgc,dgc->td",
        dgate_up.reshape(LEN, 2, hidden_units),
        ffn_in,
        preferred_element_type=f32,
    )
    dn_blocks = blocks_of(dnormed)
    ffn_in_part = transposed_times(normed2, hold(dgate_up, dn_blocks[0])).astype(bf16)
    ffn_in_sum = dp_scatter(ffn_in_part)
    columns = to_columns(
        hold(rows4, dn_blocks[0]), cotangent, low4, low3, own_picks.astype(f32)
    )
    grad, low2, gain2 = norm_backward(
        hold(grad, ffn_in_part, all_moved),
        hidden2,
        gain(1),
        split_list(dn_blocks),
    )
    grad_low2 = join_list(low2)
    grad_low2[0] = hold(grad_low2[0], columns)

    du, dzs, small, dalog, ddt, dcols_part = scan_backward(
        me, members, proj, dt_proj, bias, alog, skip, u, xz, mix_out, grad_low2, ys, states
    )
    dcols = all_sum_rows(dcols_part.astype(bf16))
    dcols = hold(dcols, attn_in_sum)
    dxs, dxproj, dconv = conv_backward(
        me, members, dcols, proj, u, xz, du, conv_weight, x_proj
    )
    dmixed = jnp.stack([dxs, dzs])
    dnormed = jnp.einsum("gtc,dgc->td", dmixed, mix_in, preferred_element_type=f32)
    dn_blocks = blocks_of(dnormed)
    mix_part = mix_grads(
        groups, normed1, hold(dxs, dn_blocks[0]), dzs, dxproj, ddt, dalog, small, dconv
    )
    mix_sum = dp_scatter(mix_part.reshape(-1, channels)).astype(f32)
    dn_blocks = split_list(dn_blocks)
    dn_blocks[0] = hold(dn_blocks[0], mix_part)
    grad, _, gain1 = norm_backward(grad, hidden1, gain(0), dn_blocks)

    columns = join_list(hold(columns, grad))
    extra = jnp.concatenate([gain1, gain2, gain3, gain4, grad_router], axis=0).astype(bf16)
    extra = jnp.pad(extra, ((0, -extra.shape[0] % 16), (0, 0)))
    last = to_columns(jnp.concatenate([low2, extra], axis=0))
    made = experts_out(members, hold(expert_low, grad), slot_weights, expert_out)
    made = hold(made[0], ffn_in_sum, *columns), *made[1:]
    sorted_rows = sorted_columns(groups, [hold(columns[0], made[0])] + columns[1:])
    part = expert_grads(0, EXPERTS // 2, all_moved, *sorted_rows)
    made = split_list([hold(made[0], part[0])] + list(made[1:]))
    hidden5 = hidden4
    for block in made:
        hidden5 = hidden5 + block.astype(f32)
    last = join_list(hold(last, part[0]))
    columns[0] = hold(columns[0], part[0])
    attn_out_sum, ffn_out_sum = out_grads(groups, 2, columns, all_attended, all_acted)
    last[0] = hold(last[0], ffn_out_sum)
    mix_out_sum, model_sum = last_grads(groups, last, all_gated)
    expert_in_grad, expert_out_grad = expert_grads(
        EXPERTS // 2,
        EXPERTS // 2,
        hold(all_moved, mix_out_sum, hidden5),
        *sorted_rows,
        earlier=part,
    )

    def padded(count):
        return count + -count % 16

    slice_of = channels // groups
    xproj_rows, dt_rows = 128 // groups, DT_RANK // groups
    dt_at = 2 * width + padded(xproj_rows)
    flat = mix_sum[dt_at + padded(dt_rows) :, :slice_of]
    heads_cols = attn_query.shape[1]
    attn_in = attn_in_sum.astype(f32)
    return (
        hidden5.astype(bf16),
        grad,
        model_sum[:4],
        jnp.stack([mix_sum[:width], mix_sum[width : 2 * width]], axis=1),
        flat[2 * STATE : 2 * STATE + CONV],
        mix_sum[2 * width : 2 * width + xproj_rows].T,
        mix_sum[dt_at : dt_at + dt_rows],
        flat[STATE],
        flat[:STATE].T,
        flat[STATE + 1],
        mix_out_sum.T,
        ffn_in_sum.astype(f32).reshape(width, 2, hidden_units),
        ffn_out_sum.T,
        attn_in[:, :heads_cols],
        attn_in[:, heads_cols:].reshape(-1, 2, attn_keyval.shape[2]),
        attn_out_sum.T,
        model_sum[4 : 4 + EXPERTS].T,
        expert_in_grad,
        expert_out_grad.transpose(0, 2, 1),
    )


def solution(mesh):
    return jax.shard_map(
        shards,
        mesh=mesh,
        in_specs=(
            P(("dp", "tensor"), None),
            P(("dp", "tensor"), None),
            P(),
            P(None, None, "tensor"),
            P(None, "tensor"),
            P("tensor", None),
            P(None, "tensor"),
            P("tensor"),
            P("tensor", None),
            P("tensor"),
            P("tensor", None),
            P(None, None, "tensor"),
            P("tensor", None),
            P(None, "tensor"),
            P(None, None, "tensor"),
            P("tensor", None),
            P(),
            P(None, None, None, "tensor"),
            P(None, "tensor", None),
            P("dp", None),
        ),
        out_specs=(
            P(("dp", "tensor"), None),
            P(("dp", "tensor"), None),
            P(None, "dp"),
            P("dp", None, "tensor"),
            P(None, ("tensor", "dp")),
            P("tensor", "dp"),
            P("dp", "tensor"),
            P(("tensor", "dp")),
            P(("tensor", "dp"), None),
            P(("tensor", "dp")),
            P("tensor", "dp"),
            P("dp", None, "tensor"),
            P("tensor", "dp"),
            P("dp", "tensor"),
            P("dp", None, "tensor"),
            P("tensor", "dp"),
            P("dp", None),
            P(None, "dp", None, "tensor"),
            P(None, "tensor", "dp"),
        ),
        check_vma=False,
    )
```

profile of v0, /device:TPU:0, one launch (start us, length us, event | category | flops | bytes accessed | tf_op | source)
XLA Modules:
  0.0 479.6 jit_solution(11516137195348622914)
XLA Ops:
  17.8 8.2 %collective-permute-done = bf16[64,1536]{1,0:T(8,128)(2,1)} collective-permute-done((bf16[64,1536]{1,0:T(8,128)(2,1)}, bf16[64,1536]{1,0:T(8,128)(2,1)}, u32[]{:S(2)}, u32[]{:S(2)}) %collective-permute-start) | collective-permute-done | bytes 196640 | tf_op jit(solution)/shard_map/ppermute | solution.py:1285
  27.0 5.2 %fusion.23.xz_ref = f32[2,256,768]{2,1,0:T(8,128)} fusion(bf16[1536,2,768]{2,1,0:T(2,128)(2,1)} %param.23, bf16[256,1536]{1,0:T(8,128)(2,1)S(1)} %constant_dynamic-update-slice_fusion.normed_ref), kind=kOutput, calls=%fused_computation.17 | convolution fusion | flops 1207959552 | bytes 7077888 | tf_op jit(solution)/shard_map/td,dgc->gtc/dot_general | solution.py:1334
  46.5 12.5 %scan_forward.1 = (bf16[256,768]{1,0:T(8,128)(2,1)}, f32[256,768]{1,0:T(8,128)}, bf16[4096,768]{1,0:T(8,128)(2,1)}, bf16[64,1536]{1,0:T(8,128)(2,1)}, bf16[64,15...) custom-call(s32[1]{0:T(128)} %bitcast.me_ref, f32[256,128]{1,0:T(8,128)} %fusion.45.proj_ref, ...), custom_call_target="tpu_custom_call" | custom-call | flops 14949999616 | bytes 1048576 | tf_op jit(solution)/shard_map/scan_forward/pallas_call | solution.py:485
  82.7 5.3 %fusion.20 = f32[2,256,1024]{2,1,0:T(8,128)S(1)} fusion(bf16[1536,2,1024]{2,1,0:T(2,128)(2,1)} %param.31, bf16[256,1536]{1,0:T(8,128)(2,1)S(1)} %constant_dynamic-update-slice_fusion.4), kind=kOutput, calls=%fused_computation.16 | convolution fusion | flops 1610612736 | bytes 9175040 | tf_op jit(solution)/shard_map/td,dgc->gtc/dot_general | solution.py:1343
  114.8 6.1 %attention_forward.1 = (bf16[256,1536]{1,0:T(8,128)(2,1)}, bf16[256,384]{1,0:T(8,128)(2,1)}, bf16[256,256]{1,0:T(8,128)(2,1)}, bf16[256,384]{1,0:T(8,128)(2,1)},...) custom-call(s32[1]{0:T(128)} %bitcast.me_ref, ...), custom_call_target="tpu_custom_call" | custom-call | flops 6899999744 | bytes 1048576 | tf_op jit(solution)/shard_map/attention_forward/pallas_call | solution.py:707
  129.8 6.4 %collective-permute-done.19.rest_2_ = bf16[64,1536]{1,0:T(8,128)(2,1)} collective-permute-done((bf16[64,1536]{1,0:T(8,128)(2,1)}, bf16[64,1536]{1,0:T(8,128)(2,1)}, u32[]{:S(2)}, u32[]{:S(2)}) %collective-permute-start.19) | collective-permute-done | bytes 196640 | tf_op jit(solution)/shard_map/ppermute | solution.py:1285
  146.6 36.4 %experts.1 = (bf16[256,1536]{1,0:T(8,128)(2,1)}, bf16[16,48,256]{2,1,0:T(8,128)(2,1)}, bf16[768,256]{1,0:T(8,128)(2,1)}, bf16[64,1664]{1,0:T(8,128)(2,1)}, bf16[...) custom-call(s32[2,256]{1,0:T(2,128)} %bitcast.97, bf16[16,1536]{1,0:T(8,128)(2,1)} %bitcast.100, ...), custom_call_target="tpu_custom_call" | custom-call | flops 42550001664 | bytes 1048576 | tf_op jit(solution)/shard_map/experts/pallas_call | solution.py:974
  183.0 8.7 %reduce-scatter.4.cloned.1.call-start = ((), (), s32[]{:S(2)}) async-start(), calls=%async_computation.9 | async-start | bytes 2211840 | tf_op jit(solution)/shard_map/reduce_scatter | solution.py:1314
  198.0 5.9 %collective-permute-done.28.rest_2_ = bf16[64,1664]{1,0:T(8,128)(2,1)} collective-permute-done((bf16[64,1664]{1,0:T(8,128)(2,1)}, bf16[64,1664]{1,0:T(8,128)(2,1)}, u32[]{:S(2)}, u32[]{:S(2)}) %collective-permute-start.28) | collective-permute-done | bytes 213024 | tf_op jit(solution)/shard_map/ppermute | solution.py:1285
  216.6 7.8 %attention_backward.1 = (bf16[256,640]{1,0:T(8,128)(2,1)}, bf16[64,1536]{1,0:T(8,128)(2,1)}, bf16[64,1536]{1,0:T(8,128)(2,1)}, bf16[64,1536]{1,0:T(8,128)(2,1)}, bf16[64,1536]{1,0:T(8,128)(2,1)}) custom-call(s32[1]{0:T(128)} %bitcast.me_ref, bf16[256,384]{1,0:T(8,128)(2,1)} %get-tuple-element.140.q_ref, bf16[256,256]{1,0:T(8,128)(2,1)} %get-tuple-element.141.kv_ref, ...), custom_call_target="tpu_custom_call" | custom-call | flops 9200000000 | bytes 1048576 | tf_op jit(solution)/shard_map/attention_backward/pallas_call | solution.py:723
  234.9 5.3 %collective-permute-done.34.rest_2_ = bf16[64,1536]{1,0:T(8,128)(2,1)S(1)} collective-permute-done((bf16[64,1536]{1,0:T(8,128)(2,1)S(1)}, bf16[64,1536]{1,0:T(8,128)(2,1)S(1)}, u32[]{:S(2)}, u32[]{:S(2)}) %collective-permute-start.34) | collective-permute-done | bytes 196640 | tf_op jit(solution)/shard_map/ppermute | solution.py:1285
  258.0 4.5 convolution_convert_fusion
  265.6 5.0 %all-to-all-start = ((bf16[8,64,896]{2,1,0:T(8,128)(2,1)}), bf16[8,64,896]{2,1,0:T(8,128)(2,1)S(1)}, u32[]{:S(2)}, u32[]{:S(2)}) async-start(bf16[8,64,896]{2,1,0:T(8,128)(2,1)} %pack_columns.2), calls=%async_computation | async-start | bytes 1835008 | tf_op jit(solution)/shard_map/all_to_all | solution.py:1320
  274.5 5.2 %collective-permute-done.41.rest_3_ = bf16[64,1536]{1,0:T(8,128)(2,1)S(1)} collective-permute-done((bf16[64,1536]{1,0:T(8,128)(2,1)S(1)}, bf16[64,1536]{1,0:T(8,128)(2,1)S(1)}, u32[]{:S(2)}, u32[]{:S(2)}) %collective-permute-start.41) | collective-permute-done | bytes 196640 | tf_op jit(solution)/shard_map/ppermute | solution.py:1285
  290.5 9.0 %all-to-all-done = bf16[8,64,896]{2,1,0:T(8,128)(2,1)S(1)} async-done(((bf16[8,64,896]{2,1,0:T(8,128)(2,1)}), bf16[8,64,896]{2,1,0:T(8,128)(2,1)S(1)}, u32[]{:S(2)}, u32[]{:S(2)}) %all-to-all-start) | async-done | bytes 917536 | tf_op jit(solution)/shard_map/all_to_all | solution.py:1320
  300.4 20.7 %scan_backward.1 = (f32[256,768]{1,0:T(8,128)}, bf16[256,768]{1,0:T(8,128)(2,1)}, f32[8,768]{1,0:T(8,128)}, f32[16,768]{1,0:T(8,128)}, f32[96,768]{1,0:T(8,128)}, /*index=5*/f32[256,128]{1,0:T(8,128)}) custom-call(s32[1]{0:T(128)} %bitcast.me_ref, f32[256,128]{1,0:T(8,128)} %fusion.45.proj_ref, bf16[96,768]{1,0:T(8,128)(2,1)} %dt_proj_ref.3, ...), custom_call_target="tpu_custom_call" | custom-call | flops 24149999616 | bytes 1048576 | tf_op jit(solution)/shard_map/scan_backward/pallas_call | solution.py:531
  331.4 5.2 %conv_backward.1 = (bf16[256,768]{1,0:T(8,128)(2,1)}, f32[128,768]{1,0:T(8,128)}, f32[4,768]{1,0:T(4,128)}) custom-call(s32[1]{0:T(128)} %bitcast.me_ref, f32[256,128]{1,0:T(8,128)} %convert_add_fusion.1.dcols_ref, f32[256,128]{1,0:T(8,128)} %fusion.45.proj_ref, f32[256,768]{1,0:T(8,128)} %get-tuple-element.114.u_ref, f32[2,256,768]{2,1,0:T(8,128)} %fusion.23.xz_ref, ...), custom_call_target="tpu_custom_call" | custom-call | flops 5750000128 | bytes 1048576 | tf_op jit(solution)/shard_map/conv_backward/pallas_call | solution.py:589
  341.3 5.4 %mix_grads.1 = bf16[8,464,768]{2,1,0:T(8,128)(2,1)} custom-call(bf16[256,1536]{1,0:T(8,128)(2,1)} %copy-done.16, bf16[256,768]{1,0:T(8,128)(2,1)} %get-tuple-element.165.first_ref, bf16[256,768]{1,0:T(8,128)(2,1)} %get-tuple-element.164.second_ref, f32[128,768]{1,0:T(8,128)} %get-tuple-element.166.refs_0_, f32[96,768]{1,0:T(8,128)} %get-tuple-element.167.refs_1_, ...), custom_call_target="tpu_custom_call" | custom-call | flops 8049999872 | bytes 1048576 | tf_op jit(solution)/shard_map/mix_grads/pallas_call | solution.py:1186
  371.6 13.7 %experts_out.1 = (bf16[64,1536]{1,0:T(8,128)(2,1)}, bf16[64,1536]{1,0:T(8,128)(2,1)}, bf16[64,1536]{1,0:T(8,128)(2,1)}, bf16[64,1536]{1,0:T(8,128)(2,1)}) custom-call(bf16[16,48,256]{2,1,0:T(8,128)(2,1)} %get-tuple-element.173.act_ref, bf16[768,256]{1,0:T(8,128)(2,1)} %get-tuple-element.174.weighted_ref, bf16[16,256,1536]{2,1,0:T(8,128)(2,1)} %w_out_ref.3), custom_call_target="tpu_custom_call" | custom-call | flops 16099999744 | bytes 1048576 | tf_op jit(solution)/shard_map/experts_out/pallas_call | solution.py:1030
  388.8 14.4 %collective-permute-done.52.refs_2_.rest_2_ = bf16[512,896]{1,0:T(8,128)(2,1)} collective-permute-done((bf16[512,896]{1,0:T(8,128)(2,1)S(1)}, bf16[512,896]{1,0:T(8,128)(2,1)}, u32[]{:S(2)}, u32[]{:S(2)}) %collective-permute-start.52) | collective-permute-done | bytes 917536 | tf_op jit(solution)/shard_map/ppermute | solution.py:1285
  408.2 14.0 %expert_grads.2 = (f32[16,192,2,256]{3,2,1,0:T(2,128)}, f32[16,192,256]{2,1,0:T(8,128)}) custom-call(bf16[2048,1536]{1,0:T(8,128)(2,1)} %all-gather.11.cloned.1.call-done.moved_ref, bf16[192,2048]{1,0:T(8,128)(2,1)} %get-tuple-element.179.left_ref, bf16[192,2048]{1,0:T(8,128)(2,1)} %get-tuple-element.180.right_ref, f32[2048,2]{1,0:T(8,128)} %get-tuple-element.181.picks_ref), custom_call_target="tpu_custom_call" | custom-call | flops 13799999488 | bytes 1048576 | tf_op jit(solution)/shard_map/expert_grads/pallas_call | solution.py:1097
  424.5 6.6 %out_grads.1 = (f32[192,384]{1,0:T(8,128)}, f32[192,1024]{1,0:T(8,128)}) custom-call(bf16[2048,384]{1,0:T(8,128)(2,1)} %all-gather.9.cloned.1.call-done.heads_ref, bf16[2048,1024]{1,0:T(8,128)(2,1)} %all-gather.7.cloned.1.call-done.acted_ref, bf16[512,896]{1,0:T(8,128)(2,1)} %bitcast.87, bf16[512,896]{1,0:T(8,128)(2,1)} %collective-permute-done.51.refs_1_.rest_1_, ...), custom_call_target="tpu_custom_call" | custom-call | flops 6899999744 | bytes 1048576 | tf_op jit(solution)/shard_map/out_grads/pallas_call | solution.py:1210
  435.7 5.7 %collective-permute-done.58.rest_2_ = bf16[768,192]{1,0:T(8,128)(2,1)S(1)} collective-permute-done((bf16[768,192]{1,0:T(8,128)(2,1)S(1)}, bf16[768,192]{1,0:T(8,128)(2,1)S(1)}, u32[]{:S(2)}, u32[]{:S(2)}) %collective-permute-start.58) | collective-permute-done | bytes 294944 | tf_op jit(solution)/shard_map/ppermute | solution.py:1285
  450.8 13.9 %expert_grads.3 = (f32[16,192,2,256]{3,2,1,0:T(2,128)}, f32[16,192,256]{2,1,0:T(8,128)}) custom-call(bf16[2048,1536]{1,0:T(8,128)(2,1)} %all-gather.11.cloned.1.call-done.moved_ref, bf16[192,2048]{1,0:T(8,128)(2,1)} %get-tuple-element.179.left_ref, bf16[192,2048]{1,0:T(8,128)(2,1)} %get-tuple-element.180.right_ref, ...), custom_call_target="tpu_custom_call", output_to_operand_aliasing={{0}: (4, {}), {1}: (5, {})} | custom-call | flops 13799999488 | bytes 1048576 | tf_op jit(solution)/shard_map/expert_grads/pallas_call | solution.py:1097
  (324 shorter events, 233.7 us)
Async XLA Ops:
  7.2 102.5 %all-gather.5.cloned.1.call-start = ((), (), s32[]{:S(2)}) async-start(), calls=%async_computation.5 | async-start | bytes 3538944 | tf_op jit(solution)/shard_map/all_gather | solution.py:1317
  12.3 14.6 %collective-permute-start.2 = (bf16[64,1536]{1,0:T(8,128)(2,1)}, bf16[64,1536]{1,0:T(8,128)(2,1)S(1)}, u32[]{:S(2)}, u32[]{:S(2)}) collective-permute-start(bf16[64,1536]{1,0:T(8,128)(2,1)} %get-tuple-element.112), channel_id=1, source_target_pairs={{0,3},{1,2},{2,1},{3,0},{4,7},{5,6},{6,5},{7,4},{8,11},{9,10},{10,... | collective-permute-start | bytes 589832 | tf_op jit(solution)/shard_map/ppermute | solution.py:1285
  59.1 136.9 %all-gather.7.cloned.1.call-start = ((), (), s32[]{:S(2)}) async-start(), calls=%async_computation.6 | async-start | bytes 4718592 | tf_op jit(solution)/shard_map/all_gather | solution.py:1317
  90.4 105.6 %all-gather.9.cloned.1.call-start = ((), (), s32[]{:S(2)}) async-start(), calls=%async_computation.7 | async-start | bytes 1769472 | tf_op jit(solution)/shard_map/all_gather | solution.py:1317
  122.0 14.2 %collective-permute-start.19 = (bf16[64,1536]{1,0:T(8,128)(2,1)}, bf16[64,1536]{1,0:T(8,128)(2,1)}, u32[]{:S(2)}, u32[]{:S(2)}) collective-permute-start(bf16[64,1536]{1,0:T(8,128)(2,1)} %get-tuple-element.127), channel_id=1, source_target_pairs={{0,2},{1,3},{2,0},{3,1},{4,6},{5,7},{6,4},{7,5},{8,10},{9,11},{10,... | collective-permute-start | bytes 589832 | tf_op jit(solution)/shard_map/ppermute | solution.py:1285
  123.3 12.8 %collective-permute-start.20 = (bf16[64,1536]{1,0:T(8,128)(2,1)}, bf16[64,1536]{1,0:T(8,128)(2,1)}, u32[]{:S(2)}, u32[]{:S(2)}) collective-permute-start(bf16[64,1536]{1,0:T(8,128)(2,1)} %get-tuple-element.128), channel_id=1, source_target_pairs={{0,3},{1,2},{2,1},{3,0},{4,7},{5,6},{6,5},{7,4},{8,11},{9,10},{10,... | collective-permute-start | bytes 589832 | tf_op jit(solution)/shard_map/ppermute | solution.py:1285
  124.4 14.7 %collective-permute-start.26 = (bf16[64,1536]{1,0:T(8,128)(2,1)S(1)}, bf16[64,1536]{1,0:T(8,128)(2,1)}, u32[]{:S(2)}, u32[]{:S(2)}) collective-permute-start(bf16[64,1536]{1,0:T(8,128)(2,1)S(1)} %copy-done.26), channel_id=1, source_target_pairs={{0,3},{1,2},{2,1},{3,0},{4,7},{5,6},{6,5},{7,4},{8,11},{9,10},{10,... | collective-permute-start | bytes 589832 | tf_op jit(solution)/shard_map/ppermute | solution.py:1285
  126.2 16.9 %collective-permute-start.25 = (bf16[64,1536]{1,0:T(8,128)(2,1)S(1)}, bf16[64,1536]{1,0:T(8,128)(2,1)}, u32[]{:S(2)}, u32[]{:S(2)}) collective-permute-start(bf16[64,1536]{1,0:T(8,128)(2,1)S(1)} %copy-done.26), channel_id=1, source_target_pairs={{0,2},{1,3},{2,0},{3,1},{4,6},{5,7},{6,4},{7,5},{8,10},{9,11},{10,... | collective-permute-start | bytes 589832 | tf_op jit(solution)/shard_map/ppermute | solution.py:1285
  128.6 14.6 %collective-permute-start.24 = (bf16[64,1536]{1,0:T(8,128)(2,1)S(1)}, bf16[64,1536]{1,0:T(8,128)(2,1)}, u32[]{:S(2)}, u32[]{:S(2)}) collective-permute-start(bf16[64,1536]{1,0:T(8,128)(2,1)S(1)} %copy-done.26), channel_id=1, source_target_pairs={{0,1},{1,0},{2,3},{3,2},{4,5},{5,4},{6,7},{7,6},{8,9},{9,8},{10,11... | collective-permute-start | bytes 589832 | tf_op jit(solution)/shard_map/ppermute | solution.py:1285
  143.1 131.4 %all-gather.11.cloned.1.call-start = ((), (), s32[]{:S(2)}) async-start(), calls=%async_computation.8 | async-start | bytes 7077888 | tf_op jit(solution)/shard_map/all_gather | solution.py:1317
  183.0 148.3 %reduce-scatter.4.cloned.1.call-start = ((), (), s32[]{:S(2)}) async-start(), calls=%async_computation.9 | async-start | bytes 2211840 | tf_op jit(solution)/shard_map/reduce_scatter | solution.py:1314
  227.5 176.5 %reduce-scatter.6.cloned.1.call-start = ((), (), s32[]{:S(2)}) async-start(), calls=%async_computation.10 | async-start | bytes 7077888 | tf_op jit(solution)/shard_map/reduce_scatter | solution.py:1314
  265.6 33.9 %all-to-all-start = ((bf16[8,64,896]{2,1,0:T(8,128)(2,1)}), bf16[8,64,896]{2,1,0:T(8,128)(2,1)S(1)}, u32[]{:S(2)}, u32[]{:S(2)}) async-start(bf16[8,64,896]{2,1,0:T(8,128)(2,1)} %pack_columns.2), calls=%async_computation | async-start | bytes 1835008 | tf_op jit(solution)/shard_map/all_to_all | solution.py:1320
  270.7 194.0 %reduce-scatter.8.cloned.1.call-start = ((), (), s32[]{:S(2)}) async-start(), calls=%async_computation.11 | async-start | bytes 6414336 | tf_op jit(solution)/shard_map/reduce_scatter | solution.py:1314
  287.0 12.5 %collective-permute-start.44 = (bf16[64,1536]{1,0:T(8,128)(2,1)}, bf16[64,1536]{1,0:T(8,128)(2,1)S(1)}, u32[]{:S(2)}, u32[]{:S(2)}) collective-permute-start(bf16[64,1536]{1,0:T(8,128)(2,1)} %get-tuple-element.159.rest_0_), channel_id=1, source_target_pairs={{0,3},{1,2},{2,1},{3,0},{4,7},{5,6},{6,5},{7,4},{8,11},{9,10},{10,... | collective-permute-start | bytes 589832 | tf_op jit(solution)/shard_map/ppermute | solution.py:1285
  360.5 26.5 %collective-permute-start.53 = (bf16[512,896]{1,0:T(8,128)(2,1)S(1)}, bf16[512,896]{1,0:T(8,128)(2,1)}, u32[]{:S(2)}, u32[]{:S(2)}) collective-permute-start(bf16[512,896]{1,0:T(8,128)(2,1)S(1)} %bitcast.83), channel_id=1, source_target_pairs={{0,3},{1,2},{2,1},{3,0},{4,7},{5,6},{6,5},{7,4},{8,11},{9,10},{10,... | collective-permute-start | bytes 2752520 | tf_op jit(solution)/shard_map/ppermute | solution.py:1285
  361.7 41.5 %collective-permute-start.52 = (bf16[512,896]{1,0:T(8,128)(2,1)S(1)}, bf16[512,896]{1,0:T(8,128)(2,1)}, u32[]{:S(2)}, u32[]{:S(2)}) collective-permute-start(bf16[512,896]{1,0:T(8,128)(2,1)S(1)} %bitcast.84), channel_id=1, source_target_pairs={{0,2},{1,3},{2,0},{3,1},{4,6},{5,7},{6,4},{7,5},{8,10},{9,11},{10,... | collective-permute-start | bytes 2752520 | tf_op jit(solution)/shard_map/ppermute | solution.py:1285
  363.0 41.0 %collective-permute-start.51 = (bf16[512,896]{1,0:T(8,128)(2,1)S(1)}, bf16[512,896]{1,0:T(8,128)(2,1)}, u32[]{:S(2)}, u32[]{:S(2)}) collective-permute-start(bf16[512,896]{1,0:T(8,128)(2,1)S(1)} %bitcast.85), channel_id=1, source_target_pairs={{0,1},{1,0},{2,3},{3,2},{4,5},{5,4},{6,7},{7,6},{8,9},{9,8},{10,11... | collective-permute-start | bytes 2752520 | tf_op jit(solution)/shard_map/ppermute | solution.py:1285
  367.5 54.7 %all-to-all-start.1 = ((bf16[8,96,192]{2,1,0:T(8,128)(2,1)}), bf16[8,96,192]{2,1,0:T(8,128)(2,1)S(1)}, u32[]{:S(2)}, u32[]{:S(2)}) async-start(bf16[8,96,192]{2,1,0:T(8,128)(2,1)} %pack_columns.3), calls=%async_computation.3 | async-start | bytes 786432 | tf_op jit(solution)/shard_map/all_to_all | solution.py:1320
  385.3 48.2 %collective-permute-start.54 = (bf16[64,1536]{1,0:T(8,128)(2,1)}, bf16[64,1536]{1,0:T(8,128)(2,1)S(1)}, u32[]{:S(2)}, u32[]{:S(2)}) collective-permute-start(bf16[64,1536]{1,0:T(8,128)(2,1)} %get-tuple-element.184), channel_id=1, source_target_pairs={{0,1},{1,0},{2,3},{3,2},{4,5},{5,4},{6,7},{7,6},{8,9},{9,8},{10,11... | collective-permute-start | bytes 589832 | tf_op jit(solution)/shard_map/ppermute | solution.py:1285
  386.3 48.6 %collective-permute-start.55 = (bf16[64,1536]{1,0:T(8,128)(2,1)}, bf16[64,1536]{1,0:T(8,128)(2,1)S(1)}, u32[]{:S(2)}, u32[]{:S(2)}) collective-permute-start(bf16[64,1536]{1,0:T(8,128)(2,1)} %get-tuple-element.185), channel_id=1, source_target_pairs={{0,2},{1,3},{2,0},{3,1},{4,6},{5,7},{6,4},{7,5},{8,10},{9,11},{10,... | collective-permute-start | bytes 589832 | tf_op jit(solution)/shard_map/ppermute | solution.py:1285
  387.0 47.9 %collective-permute-start.56 = (bf16[64,1536]{1,0:T(8,128)(2,1)}, bf16[64,1536]{1,0:T(8,128)(2,1)S(1)}, u32[]{:S(2)}, u32[]{:S(2)}) collective-permute-start(bf16[64,1536]{1,0:T(8,128)(2,1)} %get-tuple-element.186), channel_id=1, source_target_pairs={{0,3},{1,2},{2,1},{3,0},{4,7},{5,6},{6,5},{7,4},{8,11},{9,10},{10,... | collective-permute-start | bytes 589832 | tf_op jit(solution)/shard_map/ppermute | solution.py:1285
  422.2 13.5 %collective-permute-start.59 = (bf16[768,192]{1,0:T(8,128)(2,1)S(1)}, bf16[768,192]{1,0:T(8,128)(2,1)S(1)}, u32[]{:S(2)}, u32[]{:S(2)}) collective-permute-start(bf16[768,192]{1,0:T(8,128)(2,1)S(1)} %bitcast.93), channel_id=1, source_target_pairs={{0,3},{1,2},{2,1},{3,0},{4,7},{5,6},{6,5},{7,4},{8,11},{9,10},{10,... | collective-permute-start | bytes 884744 | tf_op jit(solution)/shard_map/ppermute | solution.py:1285
  423.7 17.7 %collective-permute-start.58 = (bf16[768,192]{1,0:T(8,128)(2,1)S(1)}, bf16[768,192]{1,0:T(8,128)(2,1)S(1)}, u32[]{:S(2)}, u32[]{:S(2)}) collective-permute-start(bf16[768,192]{1,0:T(8,128)(2,1)S(1)} %bitcast.94), channel_id=1, source_target_pairs={{0,2},{1,3},{2,0},{3,1},{4,6},{5,7},{6,4},{7,5},{8,10},{9,11},{10,... | collective-permute-start | bytes 884744 | tf_op jit(solution)/shard_map/ppermute | solution.py:1285
  (100 other events, 736.9 us)
Sparse Core Ops, SparseCore 0:
  59.2 38.5 all-gather.4
  100.0 46.0 all-gather.6
  147.7 23.7 all-gather.8
  183.2 64.8 all-gather.10
  250.2 37.3 reduce-scatter.3
  289.9 72.7 reduce-scatter.5
  365.1 68.9 reduce-scatter.7
where the time goes:
time: 488 us; the launch traced here: 480 us
  Pallas kernels  177 us (36%)
  waiting for transfers between devices  125 us (26%)
  starting transfers between devices  89.9 us (18%)
  local copies, waits for them, and re-layouts  33.6 us (7%)
  matrix products  28.5 us (6%)
  between operations  15.2 us (3%)
  other arithmetic  10.5 us (2%)
    ppermute x60, waiting for transfers between devices, swap(): return lax.ppermute(value, 'tensor', [(i, i ^ k) for i in range(members)])  116 us
    ppermute x60, starting transfers between devices, swap(): return lax.ppermute(value, 'tensor', [(i, i ^ k) for i in range(members)])  71.4 us
    pallas_call x1, Pallas kernels, experts(): pl.pallas_call(functools.partial(experts_kernel, blocks), grid=(EXPERTS,)...  36.4 us
    pallas_call x2, Pallas kernels, expert_grads(): pl.pallas_call(functools.partial(expert_grad_kernel, first), grid=(count,...  27.8 us
    pallas_call x1, Pallas kernels, scan_backward(): pl.pallas_call(functools.partial(scan_backward_kernel, blocks), grid=(cha...  20.7 us
    unnamed x118, local copies, waits for them, and re-layouts  14.5 us
    pallas_call x1, Pallas kernels, experts_out(): pl.pallas_call(experts_out_kernel, grid=(EXPERTS,), in_specs=[pl.BlockSpe...  13.7 us
    pallas_call x1, Pallas kernels, scan_forward(): pl.pallas_call(functools.partial(scan_forward_kernel, blocks), grid=(chan...  12.5 us
  transfers between devices with their start and end apart: 69, of which 37 were waited for; matrix products, arithmetic and copies ran while one was open for 10% of the time, Pallas kernels for 33%

commit v1 on v0

--- a/solution.py
+++ b/solution.py
@@ -1013,35 +1013,43 @@
     )(routes, router, w_in, w_out, *normed, *grad)
 
 
-def experts_out_kernel(act_ref, weighted_ref, w_out_ref, *rest):
-    made_refs, ye_ref = rest[:-1], rest[-1]
+def experts_out_kernel(blocks, act_ref, weighted_ref, w_out_ref, *rest):
+    made_refs, ye_ref = rest[-1 - blocks : -1], rest[-1]
     expert = pl.program_id(0)
     mine = pl.ds(pl.multiple_of(expert * CAP, CAP), CAP)
     ye_ref[mine, :] = matmul(act_ref[0], w_out_ref[0]).astype(bf16)
 
-    @pl.when(expert == EXPERTS - 1)
+    @pl.when(expert == pl.num_programs(0) - 1)
     def _():
-        store_blocks(made_refs, transposed_times(weighted_ref[...], ye_ref[...]))
-
-
-def experts_out(blocks, act, weighted, w_out):
+        made = transposed_times(weighted_ref[...], ye_ref[...])
+        size = LEN // blocks
+        if len(rest) > blocks + 1:
+            made = made + jnp.concatenate([ref[...].astype(f32) for ref in rest[:blocks]], axis=0)
+        for k, ref in enumerate(made_refs):
+            ref[...] = made[k * size : (k + 1) * size].astype(bf16)
+
+
+def experts_out(blocks, part, parts, act, weighted, w_out, earlier=()):
     units = w_out.shape[1]
-    slots = EXPERTS * CAP
-    return pl.pallas_call(
-        experts_out_kernel,
-        grid=(EXPERTS,),
+    count = EXPERTS // parts
+    slots = count * CAP
+    rows = whole((LEN // blocks, D))
+    return pl.pallas_call(
+        functools.partial(experts_out_kernel, blocks),
+        grid=(count,),
         in_specs=[
-            pl.BlockSpec((1, CAP, units), lambda e: (e, 0, 0)),
-            whole((slots, LEN)),
-            pl.BlockSpec((1, units, D), lambda e: (e, 0, 0)),
-        ],
-        out_specs=(whole((LEN // blocks, D)),) * blocks,
+            pl.BlockSpec((1, CAP, units), lambda e: (e + part * count, 0, 0)),
+            pl.BlockSpec((slots, LEN), lambda e: (part, 0)),
+            pl.BlockSpec((1, units, D), lambda e: (e + part * count, 0, 0)),
+        ]
+        + [rows] * len(earlier),
+        out_specs=(rows,) * blocks,
         out_shape=(shape_of((LEN // blocks, D), bf16),) * blocks,
         scratch_shapes=[pltpu.VMEM((slots, D), bf16)],
         compiler_params=params(),
-        cost_estimate=takes(14),
+        cost_estimate=takes(14 / parts),
         name="experts_out",
-    )(act, weighted, w_out)
+    )(act, weighted, w_out, *earlier)
 
 
 def sort_rows(refs, groups, out_ref):
@@ -1157,32 +1165,41 @@
     channels = grads[0].shape[1]
     share = channels // groups
     extras = [ref[...] for ref in extra_refs]
+    tall = [extra for extra in extras if extra.shape[0] > STATE]
+    flat = [extra for extra in extras if extra.shape[0] <= STATE]
     for group in range(groups):
         at = 0
         for grad in grads:
             out_ref[group, at : at + width, :] = grad[group * width : (group + 1) * width]
             at += width
-        for extra in extras:
-            if extra.shape[0] > STATE:
-                count = extra.shape[0] // groups
-                part = extra[group * count : (group + 1) * count]
-            else:
-                count = extra.shape[0]
-                part = extra[:, group * share : (group + 1) * share]
-                part = jnp.concatenate([part, jnp.zeros((count, channels - share), f32)], axis=1)
-            spare = -count % 16
-            if spare:
-                part = jnp.concatenate([part, jnp.zeros((spare, channels), f32)], axis=0)
-            out_ref[group, at : at + count + spare, :] = part.astype(bf16)
-            at += count + spare
+        rows = [
+            extra[group * (extra.shape[0] // groups) : (group + 1) * (extra.shape[0] // groups)]
+            for extra in tall
+        ]
+        line = jnp.concatenate(
+            [
+                extra[row : row + 1, group * share : (group + 1) * share]
+                for extra in flat
+                for row in range(extra.shape[0])
+            ],
+            axis=1,
+        )
+        spare = -line.shape[1] % channels
+        line = jnp.concatenate([line, jnp.zeros((1, spare), f32)], axis=1)
+        for first in range(0, line.shape[1], channels):
+            rows.append(line[:, first : first + channels])
+        spare = out_ref.shape[1] - at - sum(row.shape[0] for row in rows)
+        if spare:
+            rows.append(jnp.zeros((spare, channels), f32))
+        out_ref[group, at:, :] = jnp.concatenate(rows, axis=0).astype(bf16)
 
 
 def mix_grads(groups, normed, first, second, *extras):
     channels = first.shape[1]
-    rows = 2 * (D // groups)
-    for extra in extras:
-        count = extra.shape[0] // groups if extra.shape[0] > STATE else extra.shape[0]
-        rows += count + -count % 16
+    rows = sum(extra.shape[0] // groups for extra in extras if extra.shape[0] > STATE)
+    lines = sum(extra.shape[0] for extra in extras if extra.shape[0] <= STATE)
+    rows += -(-lines // groups)
+    rows += -rows % 16 + 2 * (D // groups)
     return pl.pallas_call(
         functools.partial(mix_grad_kernel, groups),
         grid=(1,),
@@ -1366,8 +1383,11 @@
     )
     dn_part[0] = hold(dn_part[0], all_acted, all_attended)
     all_moved = dp_gather(moved)
+    dn_part = split_list(dn_part)
+    made = experts_out(members, 0, 2, expert_low, slot_weights, expert_out)
+    dn_part[0] = hold(dn_part[0], made[0])
     grad, low4, gain4, grad_router = router_backward(
-        cotangent, hidden4, gain(3), rows4, own_picks, router_rows, split_list(dn_part)
+        cotangent, hidden4, gain(3), rows4, own_picks, router_rows, dn_part
     )
     grad_low4 = join_list(low4)
 
@@ -1378,10 +1398,12 @@
         me, members, grad_low4, query_low, keyval_low, attn_query, keyval, attn_out
     )
     dn_blocks = split_list(dnormed)
+    made = [hold(made[0], dn_blocks[0])] + list(made[1:])
+    made = experts_out(members, 1, 2, expert_low, slot_weights, expert_out, made)
     attn_in_part = transposed_times(normed3, dqkv).astype(bf16)
     attn_in_sum = dp_scatter(attn_in_part)
     grad, low3, gain3 = norm_backward(
-        hold(grad, attn_in_part), hidden3, gain(2), dn_blocks
+        hold(grad, attn_in_part, made[0]), hidden3, gain(2), dn_blocks
     )
     grad_low3 = join(low3)
 
@@ -1413,13 +1435,13 @@
         split_list(dn_blocks),
     )
     grad_low2 = join_list(low2)
-    grad_low2[0] = hold(grad_low2[0], columns)
 
     du, dzs, small, dalog, ddt, dcols_part = scan_backward(
         me, members, proj, dt_proj, bias, alog, skip, u, xz, mix_out, grad_low2, ys, states
     )
     dcols = all_sum_rows(dcols_part.astype(bf16))
-    dcols = hold(dcols, attn_in_sum)
+    dcols = hold(dcols, attn_in_sum, columns)
+    columns = join_list(hold(columns, dcols))
     dxs, dxproj, dconv = conv_backward(
         me, members, dcols, proj, u, xz, du, conv_weight, x_proj
     )
@@ -1427,20 +1449,17 @@
     dnormed = jnp.einsum("gtc,dgc->td", dmixed, mix_in, preferred_element_type=f32)
     dn_blocks = blocks_of(dnormed)
     mix_part = mix_grads(
-        groups, normed1, hold(dxs, dn_blocks[0]), dzs, dxproj, ddt, dalog, small, dconv
+        groups, normed1, hold(dxs, dn_blocks[0]), dzs, dxproj, ddt, dalog, small[:2], dconv
     )
     mix_sum = dp_scatter(mix_part.reshape(-1, channels)).astype(f32)
     dn_blocks = split_list(dn_blocks)
     dn_blocks[0] = hold(dn_blocks[0], mix_part)
     grad, _, gain1 = norm_backward(grad, hidden1, gain(0), dn_blocks)
 
-    columns = join_list(hold(columns, grad))
     extra = jnp.concatenate([gain1, gain2, gain3, gain4, grad_router], axis=0).astype(bf16)
     extra = jnp.pad(extra, ((0, -extra.shape[0] % 16), (0, 0)))
     last = to_columns(jnp.concatenate([low2, extra], axis=0))
-    made = experts_out(members, hold(expert_low, grad), slot_weights, expert_out)
-    made = hold(made[0], ffn_in_sum, *columns), *made[1:]
-    sorted_rows = sorted_columns(groups, [hold(columns[0], made[0])] + columns[1:])
+    sorted_rows = sorted_columns(groups, [hold(columns[0], grad, ffn_in_sum)] + columns[1:])
     part = expert_grads(0, EXPERTS // 2, all_moved, *sorted_rows)
     made = split_list([hold(made[0], part[0])] + list(made[1:]))
     hidden5 = hidden4
@@ -1459,13 +1478,11 @@
         earlier=part,
     )
 
-    def padded(count):
-        return count + -count % 16
-
     slice_of = channels // groups
     xproj_rows, dt_rows = 128 // groups, DT_RANK // groups
-    dt_at = 2 * width + padded(xproj_rows)
-    flat = mix_sum[dt_at + padded(dt_rows) :, :slice_of]
+    dt_at = 2 * width + xproj_rows
+    flat = mix_sum[dt_at + dt_rows :].reshape(-1)
+    flat = flat[: (STATE + 2 + CONV) * slice_of].reshape(STATE + 2 + CONV, slice_of)
     heads_cols = attn_query.shape[1]
     attn_in = attn_in_sum.astype(f32)
     return (
@@ -1473,7 +1490,7 @@
         grad,
         model_sum[:4],
         jnp.stack([mix_sum[:width], mix_sum[width : 2 * width]], axis=1),
-        flat[2 * STATE : 2 * STATE + CONV],
+        flat[STATE + 2 :],
         mix_sum[2 * width : 2 * width + xproj_rows].T,
         mix_sum[dt_at : dt_at + dt_rows],
         flat[STATE],

time: 488 us -> 467 us (0.957)
  waiting for transfers between devices: 125 us -> 106 us
  starting transfers between devices: 89.9 us -> 79.7 us
    ppermute x60, waiting for transfers between devices: 116 us -> 105 us  [swap(): return lax.ppermute(value, 'tensor', [(i, i ^ k) for i in range(members)])]
    reduce_scatter x3, starting transfers between devices: 9 us -> 0.7 us  [dp_scatter(): return lax.psum_scatter(value, 'dp', scatter_dimension=0, tiled=True)]
    all_to_all x2, waiting for transfers between devices: 9.04 us -> 1.31 us  [to_columns(): came = lax.all_to_all(pack_columns(groups, *rows), 'dp', 0, 0, tiled=True)]
    pallas_call x1 -> x2, Pallas kernels: 13.7 us -> 15.6 us  [experts_out(): pl.pallas_call(functools.partial(experts_out_kernel, blocks), grid=(count...]
    unnamed x118 -> x120, local copies, waits for them, and re-layouts: 14.5 us -> 14.4 us
  transfers between devices with their start and end apart: 69 -> 69, of which waited for: 37 -> 32; matrix products, arithmetic and copies ran while one was open for 10% -> 10% of each run, Pallas kernels for 33% -> 35%
where the time goes in v1:
time: 467 us; the launch traced here: 458 us
  Pallas kernels  180 us (39%)
  waiting for transfers between devices  106 us (23%)
  starting transfers between devices  79.7 us (17%)
  local copies, waits for them, and re-layouts  36.8 us (8%)
  matrix products  28.4 us (6%)
  between operations  15.3 us (3%)
  other arithmetic  11.7 us (3%)
    ppermute x60, waiting for transfers between devices, swap(): return lax.ppermute(value, 'tensor', [(i, i ^ k) for i in range(members)])  105 us
    ppermute x60, starting transfers between devices, swap(): return lax.ppermute(value, 'tensor', [(i, i ^ k) for i in range(members)])  70.2 us
    pallas_call x1, Pallas kernels, experts(): pl.pallas_call(functools.partial(experts_kernel, blocks), grid=(EXPERTS,)...  36.4 us
    pallas_call x2, Pallas kernels, expert_grads(): pl.pallas_call(functools.partial(expert_grad_kernel, first), grid=(count,...  27.8 us
    pallas_call x1, Pallas kernels, scan_backward(): pl.pallas_call(functools.partial(scan_backward_kernel, blocks), grid=(cha...  20.9 us
    pallas_call x2, Pallas kernels, experts_out(): pl.pallas_call(functools.partial(experts_out_kernel, blocks), grid=(count...  15.6 us
    unnamed x120, local copies, waits for them, and re-layouts  14.4 us
    pallas_call x1, Pallas kernels, scan_forward(): pl.pallas_call(functools.partial(scan_forward_kernel, blocks), grid=(chan...  12.5 us
  transfers between devices with their start and end apart: 69, of which 32 were waited for; matrix products, arithmetic and copies ran while one was open for 10% of the time, Pallas kernels for 35%

profile of v1, /device:TPU:0, one launch (start us, length us, event | category | flops | bytes accessed | tf_op | source)
XLA Modules:
  0.0 458.0 jit_solution(14671122822676500220)
XLA Ops:
  17.8 8.2 %collective-permute-done = bf16[64,1536]{1,0:T(8,128)(2,1)} collective-permute-done((bf16[64,1536]{1,0:T(8,128)(2,1)}, bf16[64,1536]{1,0:T(8,128)(2,1)}, u32[]{:S(2)}, u32[]{:S(2)}) %collective-permute-start) | collective-permute-done | bytes 196640 | tf_op jit(solution)/shard_map/ppermute | solution.py:1302
  27.0 5.2 %fusion.23.xz_ref = f32[2,256,768]{2,1,0:T(8,128)} fusion(bf16[1536,2,768]{2,1,0:T(2,128)(2,1)} %param.23, bf16[256,1536]{1,0:T(8,128)(2,1)S(1)} %constant_dynamic-update-slice_fusion.normed_ref), kind=kOutput, calls=%fused_computation.17 | convolution fusion | flops 1207959552 | bytes 7077888 | tf_op jit(solution)/shard_map/td,dgc->gtc/dot_general | solution.py:1351
  46.5 12.5 %scan_forward.1 = (bf16[256,768]{1,0:T(8,128)(2,1)}, f32[256,768]{1,0:T(8,128)}, bf16[4096,768]{1,0:T(8,128)(2,1)}, bf16[64,1536]{1,0:T(8,128)(2,1)}, bf16[64,15...) custom-call(s32[1]{0:T(128)} %bitcast.me_ref, f32[256,128]{1,0:T(8,128)} %fusion.45.proj_ref, ...), custom_call_target="tpu_custom_call" | custom-call | flops 14949999616 | bytes 1048576 | tf_op jit(solution)/shard_map/scan_forward/pallas_call | solution.py:485
  82.7 5.3 %fusion.20 = f32[2,256,1024]{2,1,0:T(8,128)S(1)} fusion(bf16[1536,2,1024]{2,1,0:T(2,128)(2,1)} %param.31, bf16[256,1536]{1,0:T(8,128)(2,1)S(1)} %constant_dynamic-update-slice_fusion.4), kind=kOutput, calls=%fused_computation.16 | convolution fusion | flops 1610612736 | bytes 9175040 | tf_op jit(solution)/shard_map/td,dgc->gtc/dot_general | solution.py:1360
  114.7 6.1 %attention_forward.1 = (bf16[256,1536]{1,0:T(8,128)(2,1)}, bf16[256,384]{1,0:T(8,128)(2,1)}, bf16[256,256]{1,0:T(8,128)(2,1)}, bf16[256,384]{1,0:T(8,128)(2,1)},...) custom-call(s32[1]{0:T(128)} %bitcast.me_ref, ...), custom_call_target="tpu_custom_call" | custom-call | flops 6899999744 | bytes 1048576 | tf_op jit(solution)/shard_map/attention_forward/pallas_call | solution.py:707
  129.7 6.4 %collective-permute-done.19.rest_2_ = bf16[64,1536]{1,0:T(8,128)(2,1)} collective-permute-done((bf16[64,1536]{1,0:T(8,128)(2,1)}, bf16[64,1536]{1,0:T(8,128)(2,1)}, u32[]{:S(2)}, u32[]{:S(2)}) %collective-permute-start.19) | collective-permute-done | bytes 196640 | tf_op jit(solution)/shard_map/ppermute | solution.py:1302
  146.6 36.4 %experts.1 = (bf16[256,1536]{1,0:T(8,128)(2,1)}, bf16[16,48,256]{2,1,0:T(8,128)(2,1)}, bf16[768,256]{1,0:T(8,128)(2,1)}, bf16[64,1664]{1,0:T(8,128)(2,1)}, bf16[...) custom-call(s32[2,256]{1,0:T(2,128)} %bitcast.93, bf16[16,1536]{1,0:T(8,128)(2,1)} %bitcast.96, ...), custom_call_target="tpu_custom_call" | custom-call | flops 42550001664 | bytes 1048576 | tf_op jit(solution)/shard_map/experts/pallas_call | solution.py:974
  187.6 7.8 %experts_out.2 = (bf16[64,1536]{1,0:T(8,128)(2,1)}, bf16[64,1536]{1,0:T(8,128)(2,1)}, bf16[64,1536]{1,0:T(8,128)(2,1)}, bf16[64,1536]{1,0:T(8,128)(2,1)}) custom-call(bf16[16,48,256]{2,1,0:T(8,128)(2,1)} %get-tuple-element.134.act_ref, bf16[768,256]{1,0:T(8,128)(2,1)} %get-tuple-element.135.weighted_ref, bf16[16,256,1536]{2,1,0:T(8,128)(2,1)} %w_out_ref.5), custom_call_target="tpu_custom_call" | custom-call | flops 8049999872 | bytes 1048576 | tf_op jit(solution)/shard_map/experts_out/pallas_call | solution.py:1037
  208.2 7.8 %attention_backward.1 = (bf16[256,640]{1,0:T(8,128)(2,1)}, bf16[64,1536]{1,0:T(8,128)(2,1)}, bf16[64,1536]{1,0:T(8,128)(2,1)}, bf16[64,1536]{1,0:T(8,128)(2,1)}, bf16[64,1536]{1,0:T(8,128)(2,1)}) custom-call(s32[1]{0:T(128)} %bitcast.me_ref, bf16[256,384]{1,0:T(8,128)(2,1)} %get-tuple-element.137.q_ref, bf16[256,256]{1,0:T(8,128)(2,1)} %get-tuple-element.138.kv_ref, ...), custom_call_target="tpu_custom_call" | custom-call | flops 9200000000 | bytes 1048576 | tf_op jit(solution)/shard_map/attention_backward/pallas_call | solution.py:723
  223.0 7.9 %experts_out.3 = (bf16[64,1536]{1,0:T(8,128)(2,1)}, bf16[64,1536]{1,0:T(8,128)(2,1)}, bf16[64,1536]{1,0:T(8,128)(2,1)}, bf16[64,1536]{1,0:T(8,128)(2,1)}) custom-call(bf16[16,48,256]{2,1,0:T(8,128)(2,1)} %get-tuple-element.134.act_ref, bf16[768,256]{1,0:T(8,128)(2,1)} %get-tuple-element.135.weighted_ref, bf16[16,256,1536]{2,1,0:T(8,128)(2,1)} %w_out_ref.5, ...), custom_call_target="tpu_custom_call" | custom-call | flops 8049999872 | bytes 1048576 | tf_op jit(solution)/shard_map/experts_out/pallas_call | solution.py:1037
  249.0 4.5 convolution_convert_fusion
  257.9 4.1 collective-permute-done.41.rest_3_
  262.0 4.5 collective-permute-done.40.rest_2_
  276.3 4.8 %all-to-all-start = ((bf16[8,64,896]{2,1,0:T(8,128)(2,1)}), bf16[8,64,896]{2,1,0:T(8,128)(2,1)S(1)}, u32[]{:S(2)}, u32[]{:S(2)}) async-start(bf16[8,64,896]{2,1,0:T(8,128)(2,1)} %pack_columns.2), calls=%async_computation | async-start | bytes 1835008 | tf_op jit(solution)/shard_map/all_to_all | solution.py:1337
  281.9 20.9 %scan_backward.1 = (f32[256,768]{1,0:T(8,128)}, bf16[256,768]{1,0:T(8,128)(2,1)}, f32[8,768]{1,0:T(8,128)}, f32[16,768]{1,0:T(8,128)}, f32[96,768]{1,0:T(8,128)}, /*index=5*/f32[256,128]{1,0:T(8,128)}) custom-call(s32[1]{0:T(128)} %bitcast.me_ref, f32[256,128]{1,0:T(8,128)} %fusion.45.proj_ref, bf16[96,768]{1,0:T(8,128)(2,1)} %dt_proj_ref.3, ...), custom_call_target="tpu_custom_call" | custom-call | flops 24149999616 | bytes 1048576 | tf_op jit(solution)/shard_map/scan_backward/pallas_call | solution.py:531
  313.8 5.6 %conv_backward.1 = (bf16[256,768]{1,0:T(8,128)(2,1)}, f32[128,768]{1,0:T(8,128)}, f32[4,768]{1,0:T(4,128)}) custom-call(s32[1]{0:T(128)} %bitcast.me_ref, f32[256,128]{1,0:T(8,128)} %convert_add_fusion.1.dcols_ref, f32[256,128]{1,0:T(8,128)} %fusion.45.proj_ref, f32[256,768]{1,0:T(8,128)} %get-tuple-element.117.u_ref, f32[2,256,768]{2,1,0:T(8,128)} %fusion.23.xz_ref, ...), custom_call_target="tpu_custom_call" | custom-call | flops 5750000128 | bytes 1048576 | tf_op jit(solution)/shard_map/conv_backward/pallas_call | solution.py:589
  324.0 5.2 %mix_grads.1 = bf16[8,416,768]{2,1,0:T(8,128)(2,1)} custom-call(bf16[256,1536]{1,0:T(8,128)(2,1)} %copy-done.16, bf16[256,768]{1,0:T(8,128)(2,1)} %get-tuple-element.176.first_ref, bf16[256,768]{1,0:T(8,128)(2,1)} %get-tuple-element.175.second_ref, f32[128,768]{1,0:T(8,128)} %get-tuple-element.177.refs_0_, f32[96,768]{1,0:T(8,128)} %get-tuple-element.178.refs_1_, ...), custom_call_target="tpu_custom_call" | custom-call | flops 8049999872 | bytes 1048576 | tf_op jit(solution)/shard_map/mix_grads/pallas_call | solution.py:1203
  339.9 17.2 %collective-permute-done.49.rest_2_ = bf16[64,1536]{1,0:T(8,128)(2,1)S(1)} collective-permute-done((bf16[64,1536]{1,0:T(8,128)(2,1)S(1)}, bf16[64,1536]{1,0:T(8,128)(2,1)S(1)}, u32[]{:S(2)}, u32[]{:S(2)}) %collective-permute-start.49) | collective-permute-done | bytes 196640 | tf_op jit(solution)/shard_map/ppermute | solution.py:1302
  371.4 8.0 %collective-permute-done.52.refs_2_.rest_2_ = bf16[512,896]{1,0:T(8,128)(2,1)} collective-permute-done((bf16[512,896]{1,0:T(8,128)(2,1)S(1)}, bf16[512,896]{1,0:T(8,128)(2,1)}, u32[]{:S(2)}, u32[]{:S(2)}) %collective-permute-start.52) | collective-permute-done | bytes 917536 | tf_op jit(solution)/shard_map/ppermute | solution.py:1302
  380.7 4.2 sorted_columns.1
  384.9 13.9 %expert_grads.2 = (f32[16,192,2,256]{3,2,1,0:T(2,128)}, f32[16,192,256]{2,1,0:T(8,128)}) custom-call(bf16[2048,1536]{1,0:T(8,128)(2,1)} %all-gather.11.cloned.1.call-done.moved_ref, bf16[192,2048]{1,0:T(8,128)(2,1)} %get-tuple-element.185.left_ref, bf16[192,2048]{1,0:T(8,128)(2,1)} %get-tuple-element.186.right_ref, f32[2048,2]{1,0:T(8,128)} %get-tuple-element.187.picks_ref), custom_call_target="tpu_custom_call" | custom-call | flops 13799999488 | bytes 1048576 | tf_op jit(solution)/shard_map/expert_grads/pallas_call | solution.py:1105
  401.2 6.7 %out_grads.1 = (f32[192,384]{1,0:T(8,128)}, f32[192,1024]{1,0:T(8,128)}) custom-call(bf16[2048,384]{1,0:T(8,128)(2,1)} %all-gather.9.cloned.1.call-done.heads_ref, bf16[2048,1024]{1,0:T(8,128)(2,1)} %all-gather.7.cloned.1.call-done.acted_ref, bf16[512,896]{1,0:T(8,128)(2,1)} %bitcast.82, bf16[512,896]{1,0:T(8,128)(2,1)} %collective-permute-done.51.refs_1_.rest_1_, ...), custom_call_target="tpu_custom_call" | custom-call | flops 6899999744 | bytes 1048576 | tf_op jit(solution)/shard_map/out_grads/pallas_call | solution.py:1227
  412.4 4.4 collective-permute-done.58.rest_2_
  425.9 13.9 %expert_grads.3 = (f32[16,192,2,256]{3,2,1,0:T(2,128)}, f32[16,192,256]{2,1,0:T(8,128)}) custom-call(bf16[2048,1536]{1,0:T(8,128)(2,1)} %all-gather.11.cloned.1.call-done.moved_ref, bf16[192,2048]{1,0:T(8,128)(2,1)} %get-tuple-element.185.left_ref, bf16[192,2048]{1,0:T(8,128)(2,1)} %get-tuple-element.186.right_ref, ...), custom_call_target="tpu_custom_call", output_to_operand_aliasing={{0}: (4, {}), {1}: (5, {})} | custom-call | flops 13799999488 | bytes 1048576 | tf_op jit(solution)/shard_map/expert_grads/pallas_call | solution.py:1105
  (332 shorter events, 221.4 us)
Async XLA Ops:
  7.2 102.5 %all-gather.5.cloned.1.call-start = ((), (), s32[]{:S(2)}) async-start(), calls=%async_computation.5 | async-start | bytes 3538944 | tf_op jit(solution)/shard_map/all_gather | solution.py:1334
  12.3 14.6 %collective-permute-start.2 = (bf16[64,1536]{1,0:T(8,128)(2,1)}, bf16[64,1536]{1,0:T(8,128)(2,1)S(1)}, u32[]{:S(2)}, u32[]{:S(2)}) collective-permute-start(bf16[64,1536]{1,0:T(8,128)(2,1)} %get-tuple-element.115), channel_id=1, source_target_pairs={{0,3},{1,2},{2,1},{3,0},{4,7},{5,6},{6,5},{7,4},{8,11},{9,10},{10,... | collective-permute-start | bytes 589832 | tf_op jit(solution)/shard_map/ppermute | solution.py:1302
  59.1 136.3 %all-gather.7.cloned.1.call-start = ((), (), s32[]{:S(2)}) async-start(), calls=%async_computation.6 | async-start | bytes 4718592 | tf_op jit(solution)/shard_map/all_gather | solution.py:1334
  90.4 105.0 %all-gather.9.cloned.1.call-start = ((), (), s32[]{:S(2)}) async-start(), calls=%async_computation.7 | async-start | bytes 1769472 | tf_op jit(solution)/shard_map/all_gather | solution.py:1334
  121.9 14.2 %collective-permute-start.19 = (bf16[64,1536]{1,0:T(8,128)(2,1)}, bf16[64,1536]{1,0:T(8,128)(2,1)}, u32[]{:S(2)}, u32[]{:S(2)}) collective-permute-start(bf16[64,1536]{1,0:T(8,128)(2,1)} %get-tuple-element.130), channel_id=1, source_target_pairs={{0,2},{1,3},{2,0},{3,1},{4,6},{5,7},{6,4},{7,5},{8,10},{9,11},{10,... | collective-permute-start | bytes 589832 | tf_op jit(solution)/shard_map/ppermute | solution.py:1302
  124.3 14.6 %collective-permute-start.26 = (bf16[64,1536]{1,0:T(8,128)(2,1)S(1)}, bf16[64,1536]{1,0:T(8,128)(2,1)}, u32[]{:S(2)}, u32[]{:S(2)}) collective-permute-start(bf16[64,1536]{1,0:T(8,128)(2,1)S(1)} %copy-done.26), channel_id=1, source_target_pairs={{0,3},{1,2},{2,1},{3,0},{4,7},{5,6},{6,5},{7,4},{8,11},{9,10},{10,... | collective-permute-start | bytes 589832 | tf_op jit(solution)/shard_map/ppermute | solution.py:1302
  126.2 17.0 %collective-permute-start.25 = (bf16[64,1536]{1,0:T(8,128)(2,1)S(1)}, bf16[64,1536]{1,0:T(8,128)(2,1)}, u32[]{:S(2)}, u32[]{:S(2)}) collective-permute-start(bf16[64,1536]{1,0:T(8,128)(2,1)S(1)} %copy-done.26), channel_id=1, source_target_pairs={{0,2},{1,3},{2,0},{3,1},{4,6},{5,7},{6,4},{7,5},{8,10},{9,11},{10,... | collective-permute-start | bytes 589832 | tf_op jit(solution)/shard_map/ppermute | solution.py:1302
  128.5 14.6 %collective-permute-start.24 = (bf16[64,1536]{1,0:T(8,128)(2,1)S(1)}, bf16[64,1536]{1,0:T(8,128)(2,1)}, u32[]{:S(2)}, u32[]{:S(2)}) collective-permute-start(bf16[64,1536]{1,0:T(8,128)(2,1)S(1)} %copy-done.26), channel_id=1, source_target_pairs={{0,1},{1,0},{2,3},{3,2},{4,5},{5,4},{6,7},{7,6},{8,9},{9,8},{10,11... | collective-permute-start | bytes 589832 | tf_op jit(solution)/shard_map/ppermute | solution.py:1302
  143.1 114.8 %all-gather.11.cloned.1.call-start = ((), (), s32[]{:S(2)}) async-start(), calls=%async_computation.8 | async-start | bytes 7077888 | tf_op jit(solution)/shard_map/all_gather | solution.py:1334
  182.9 130.8 %reduce-scatter.4.cloned.1.call-start = ((), (), s32[]{:S(2)}) async-start(), calls=%async_computation.9 | async-start | bytes 2211840 | tf_op jit(solution)/shard_map/reduce_scatter | solution.py:1331
  219.2 151.2 %reduce-scatter.6.cloned.1.call-start = ((), (), s32[]{:S(2)}) async-start(), calls=%async_computation.10 | async-start | bytes 7077888 | tf_op jit(solution)/shard_map/reduce_scatter | solution.py:1331
  276.3 37.5 %all-to-all-start = ((bf16[8,64,896]{2,1,0:T(8,128)(2,1)}), bf16[8,64,896]{2,1,0:T(8,128)(2,1)S(1)}, u32[]{:S(2)}, u32[]{:S(2)}) async-start(bf16[8,64,896]{2,1,0:T(8,128)(2,1)} %pack_columns.2), calls=%async_computation | async-start | bytes 1835008 | tf_op jit(solution)/shard_map/all_to_all | solution.py:1337
  281.1 158.7 %reduce-scatter.8.cloned.1.call-start = ((), (), s32[]{:S(2)}) async-start(), calls=%async_computation.11 | async-start | bytes 5750784 | tf_op jit(solution)/shard_map/reduce_scatter | solution.py:1331
  330.0 27.1 %collective-permute-start.49 = (bf16[64,1536]{1,0:T(8,128)(2,1)S(1)}, bf16[64,1536]{1,0:T(8,128)(2,1)S(1)}, u32[]{:S(2)}, u32[]{:S(2)}) collective-permute-start(bf16[64,1536]{1,0:T(8,128)(2,1)S(1)} %get-tuple-element.290), channel_id=1, source_target_pairs={{0,2},{1,3},{2,0},{3,1},{4,6},{5,7},{6,4},{7,5},{8,10},{9,11},{10,... | collective-permute-start | bytes 589832 | tf_op jit(solution)/shard_map/ppermute | solution.py:1302
  330.9 27.9 %collective-permute-start.48 = (bf16[64,1536]{1,0:T(8,128)(2,1)S(1)}, bf16[64,1536]{1,0:T(8,128)(2,1)S(1)}, u32[]{:S(2)}, u32[]{:S(2)}) collective-permute-start(bf16[64,1536]{1,0:T(8,128)(2,1)S(1)} %get-tuple-element.291), channel_id=1, source_target_pairs={{0,1},{1,0},{2,3},{3,2},{4,5},{5,4},{6,7},{7,6},{8,9},{9,8},{10,11... | collective-permute-start | bytes 589832 | tf_op jit(solution)/shard_map/ppermute | solution.py:1302
  332.9 37.5 %collective-permute-start.53 = (bf16[512,896]{1,0:T(8,128)(2,1)S(1)}, bf16[512,896]{1,0:T(8,128)(2,1)}, u32[]{:S(2)}, u32[]{:S(2)}) collective-permute-start(bf16[512,896]{1,0:T(8,128)(2,1)S(1)} %bitcast.78), channel_id=1, source_target_pairs={{0,3},{1,2},{2,1},{3,0},{4,7},{5,6},{6,5},{7,4},{8,11},{9,10},{10,... | collective-permute-start | bytes 2752520 | tf_op jit(solution)/shard_map/ppermute | solution.py:1302
  333.5 45.8 %collective-permute-start.52 = (bf16[512,896]{1,0:T(8,128)(2,1)S(1)}, bf16[512,896]{1,0:T(8,128)(2,1)}, u32[]{:S(2)}, u32[]{:S(2)}) collective-permute-start(bf16[512,896]{1,0:T(8,128)(2,1)S(1)} %bitcast.79), channel_id=1, source_target_pairs={{0,2},{1,3},{2,0},{3,1},{4,6},{5,7},{6,4},{7,5},{8,10},{9,11},{10,... | collective-permute-start | bytes 2752520 | tf_op jit(solution)/shard_map/ppermute | solution.py:1302
  338.2 42.4 %collective-permute-start.51 = (bf16[512,896]{1,0:T(8,128)(2,1)S(1)}, bf16[512,896]{1,0:T(8,128)(2,1)}, u32[]{:S(2)}, u32[]{:S(2)}) collective-permute-start(bf16[512,896]{1,0:T(8,128)(2,1)S(1)} %bitcast.80), channel_id=1, source_target_pairs={{0,1},{1,0},{2,3},{3,2},{4,5},{5,4},{6,7},{7,6},{8,9},{9,8},{10,11... | collective-permute-start | bytes 2752520 | tf_op jit(solution)/shard_map/ppermute | solution.py:1302
  357.1 53.3 %collective-permute-start.54 = (bf16[64,1536]{1,0:T(8,128)(2,1)}, bf16[64,1536]{1,0:T(8,128)(2,1)S(1)}, u32[]{:S(2)}, u32[]{:S(2)}) collective-permute-start(bf16[64,1536]{1,0:T(8,128)(2,1)} %get-tuple-element.190), channel_id=1, source_target_pairs={{0,1},{1,0},{2,3},{3,2},{4,5},{5,4},{6,7},{7,6},{8,9},{9,8},{10,11... | collective-permute-start | bytes 589832 | tf_op jit(solution)/shard_map/ppermute | solution.py:1302
  358.8 52.8 %collective-permute-start.55 = (bf16[64,1536]{1,0:T(8,128)(2,1)}, bf16[64,1536]{1,0:T(8,128)(2,1)S(1)}, u32[]{:S(2)}, u32[]{:S(2)}) collective-permute-start(bf16[64,1536]{1,0:T(8,128)(2,1)} %get-tuple-element.191), channel_id=1, source_target_pairs={{0,2},{1,3},{2,0},{3,1},{4,6},{5,7},{6,4},{7,5},{8,10},{9,11},{10,... | collective-permute-start | bytes 589832 | tf_op jit(solution)/shard_map/ppermute | solution.py:1302
  366.6 32.2 %all-to-all-start.1 = ((bf16[8,96,192]{2,1,0:T(8,128)(2,1)}), bf16[8,96,192]{2,1,0:T(8,128)(2,1)S(1)}, u32[]{:S(2)}, u32[]{:S(2)}) async-start(bf16[8,96,192]{2,1,0:T(8,128)(2,1)} %pack_columns.3), calls=%async_computation.3 | async-start | bytes 786432 | tf_op jit(solution)/shard_map/all_to_all | solution.py:1337
  370.4 41.2 %collective-permute-start.56 = (bf16[64,1536]{1,0:T(8,128)(2,1)S(1)}, bf16[64,1536]{1,0:T(8,128)(2,1)S(1)}, u32[]{:S(2)}, u32[]{:S(2)}) collective-permute-start(bf16[64,1536]{1,0:T(8,128)(2,1)S(1)} %copy-done.27), channel_id=1, source_target_pairs={{0,3},{1,2},{2,1},{3,0},{4,7},{5,6},{6,5},{7,4},{8,11},{9,10},{10,... | collective-permute-start | bytes 589832 | tf_op jit(solution)/shard_map/ppermute | solution.py:1302
  398.8 13.6 %collective-permute-start.59 = (bf16[768,192]{1,0:T(8,128)(2,1)S(1)}, bf16[768,192]{1,0:T(8,128)(2,1)S(1)}, u32[]{:S(2)}, u32[]{:S(2)}) collective-permute-start(bf16[768,192]{1,0:T(8,128)(2,1)S(1)} %bitcast.88), channel_id=1, source_target_pairs={{0,3},{1,2},{2,1},{3,0},{4,7},{5,6},{6,5},{7,4},{8,11},{9,10},{10,... | collective-permute-start | bytes 884744 | tf_op jit(solution)/shard_map/ppermute | solution.py:1302
  400.0 16.8 %collective-permute-start.58 = (bf16[768,192]{1,0:T(8,128)(2,1)S(1)}, bf16[768,192]{1,0:T(8,128)(2,1)S(1)}, u32[]{:S(2)}, u32[]{:S(2)}) collective-permute-start(bf16[768,192]{1,0:T(8,128)(2,1)S(1)} %bitcast.89), channel_id=1, source_target_pairs={{0,2},{1,3},{2,0},{3,1},{4,6},{5,7},{6,4},{7,5},{8,10},{9,11},{10,... | collective-permute-start | bytes 884744 | tf_op jit(solution)/shard_map/ppermute | solution.py:1302
  (101 other events, 755.6 us)
Sparse Core Ops, SparseCore 0:
  59.2 38.5 all-gather.4
  100.0 46.0 all-gather.6
  147.7 23.8 all-gather.8
  183.1 64.8 all-gather.10
  250.2 34.1 reduce-scatter.3
  286.6 74.4 reduce-scatter.5
  363.6 65.7 reduce-scatter.7
